TPU v7x, 32 devices: a whole 2x2x4 slice. The times are simulated.
32 devices in a mesh: dp: 8 (over z, core), sub: 4 (over y, x).
Axes of the slice: x: 2, y: 2, z: 4, core: 2. Of those that a mesh axis runs over, the one named last changes fastest.
Arguments:
- samples: bfloat16 [4096, 256], P(('dp', 'sub')), may hold values from -12 to 12
- rotation: bfloat16 [256, 256], P(None, 'sub'), may hold values from -0.375 to 0.375
- codebook: float32 [4, 256, 64], P('sub'), may hold values from -4 to 4
Outputs:
- recon: bfloat16 [4096, 256], P(('dp', 'sub'))
- new_codebook: float32 [4, 256, 64], P('sub')
- cross: float32 [256, 256], P(('dp', 'sub'))
All inputs are finite; a program needn't handle non-finite values.
Results may differ from a plain program's by a relative error of at most 0.02.
Values may be sent and summed in bfloat16 or wider, within the bound.
A program may use at most 64 MiB of HBM per device.

v0:
```python
import jax
import jax.numpy as jnp
from jax import lax
from jax.sharding import PartitionSpec as P


def per_device(samples, rotation, codebook):
    full_rotation = lax.all_gather(rotation, "sub", axis=1, tiled=True)
    rotated = jnp.dot(samples, full_rotation, preferred_element_type=jnp.float32).astype(
        jnp.bfloat16
    )
    grouped = lax.all_to_all(rotated, "sub", split_axis=1, concat_axis=0, tiled=True)
    group_rows = grouped.shape[0]
    sub_width = grouped.shape[1]
    code_count = codebook.shape[1]
    block_rows = min(2048, group_rows)
    count_blocks = group_rows // block_rows
    codes_low = codebook[0].astype(jnp.bfloat16)
    code_square = jnp.sum(codebook[0] * codebook[0], axis=-1)

    def assign(carry, block):
        sums, counts = carry
        inner = lax.dot_general(
            block, codes_low, (((1,), (1,)), ((), ())), preferred_element_type=jnp.float32
        )
        block_wide = block.astype(jnp.float32)
        row_square = jnp.sum(block_wide * block_wide, axis=-1, keepdims=True)
        logits = -0.125 * (row_square - 2.0 * inner + code_square[None])
        weights = jax.nn.softmax(logits, axis=-1).astype(jnp.bfloat16)
        rebuilt = jnp.dot(weights, codes_low, preferred_element_type=jnp.float32).astype(
            jnp.bfloat16
        )
        sums = sums + lax.dot_general(
            weights, block, (((0,), (0,)), ((), ())), preferred_element_type=jnp.float32
        )
        counts = counts + jnp.sum(weights.astype(jnp.float32), axis=0)
        return ((sums, counts), rebuilt)

    start = (jnp.zeros((code_count, sub_width), jnp.float32), jnp.zeros((code_count,), jnp.float32))
    (sums, counts), rebuilt = lax.scan(
        assign, start, grouped.reshape(count_blocks, block_rows, sub_width)
    )
    rebuilt = rebuilt.reshape(group_rows, sub_width)
    recon = lax.all_to_all(rebuilt, "sub", split_axis=0, concat_axis=1, tiled=True)
    cross = lax.psum_scatter(
        lax.dot_general(
            samples, recon, (((0,), (0,)), ((), ())), preferred_element_type=jnp.float32
        ),
        ("dp", "sub"),
        scatter_dimension=0,
        tiled=True,
    )
    sums, counts = (
        lax.psum(sums.astype(jnp.bfloat16), "dp").astype(jnp.float32),
        lax.psum(counts.astype(jnp.bfloat16), "dp").astype(jnp.float32),
    )
    new_codes = (sums + codebook[0]) / (counts[:, None] + 1.0)
    return (recon, new_codes[None], cross)


def solution(mesh):
    in_specs = (P(("dp", "sub"), None), P(None, "sub"), P("sub", None, None))
    out_specs = (P(("dp", "sub"), None), P("sub", None, None), P(("dp", "sub"), None))
    return jax.shard_map(
        per_device, mesh=mesh, in_specs=in_specs, out_specs=out_specs, check_vma=False
    )
```

profile of v0, /device:TPU:0, one launch (start us, length us, event | category | flops | bytes accessed | tf_op | source)
XLA Modules:
  0.0 181.0 jit_solution(2752701156000158753)
XLA Ops:
  7.2 0.0 copy-start
  7.2 10.2 %all_gather.3 = bf16[256,256]{0,1:T(8,128)(2,1)S(1)} all-gather(bf16[256,64]{0,1:T(8,128)(2,1)} %param.4), channel_id=1, replica_groups=mesh['dp'=8,'sub'=4] {'sub'}, dimensions={1}, use_global_device_ids=true | all-gather | bytes 163840 | tf_op jit(solution)/shard_map/all_gather | solution.py:8
  17.4 0.0 copy-done
  17.4 0.2 convolution_convert_fusion
  17.6 0.7 copy.30
  18.4 3.4 %all-to-all-start = ((bf16[128,4,64]{0,2,1:T(8,128)(2,1)}), bf16[128,4,64]{0,2,1:T(8,128)(2,1)S(1)}, u32[]{:S(2)}, u32[]{:S(2)}) async-start(bf16[128,4,64]{0,2,1:T(8,128)(2,1)} %bitcast), calls=%async_computation | async-start | bytes 131072 | tf_op jit(solution)/shard_map/all_to_all | solution.py:12
  21.8 0.0 copy-done.5
  21.8 0.1 copy.33
  21.9 0.1 multiply_reduce_fusion
  22.0 4.6 %all-to-all-done = bf16[128,4,64]{0,2,1:T(8,128)(2,1)S(1)} async-done(((bf16[128,4,64]{0,2,1:T(8,128)(2,1)}), bf16[128,4,64]{0,2,1:T(8,128)(2,1)S(1)}, u32[]{:S(2)}, u32[]{:S(2)}) %all-to-all-start) | async-done | bytes 65568 | tf_op jit(solution)/shard_map/all_to_all | solution.py:12
  26.6 0.4 fusion.11
  27.0 0.0 copy-done.3
  27.0 0.2 fusion.3
  27.3 0.5 copy-done.1
  27.8 2.3 %online-softmax = f32[512,64]{1,0:T(8,128)} custom-call(f32[512,256]{1,0:T(8,128)} %copy-done.1, f32[256,64]{1,0:T(8,128)} %bitcast.40), custom_call_target="tpu_custom_call" | custom-call | tf_op online-softmax
  30.1 1.0 convert_element_type.42
  31.2 0.7 copy.34
  31.9 3.3 %all-to-all-start.1 = ((bf16[4,128,64]{1,2,0:T(8,128)(2,1)}), bf16[4,128,64]{1,2,0:T(8,128)(2,1)S(1)}, u32[]{:S(2)}, u32[]{:S(2)}) async-start(bf16[4,128,64]{1,2,0:T(8,128)(2,1)} %copy.34), calls=%async_computation.1 | async-start | bytes 131072 | tf_op jit(solution)/shard_map/all_to_all | solution.py:44
  35.2 0.0 reduce-scatter.4.cloned.1.call-start
  35.2 0.0 copy-done.2
  35.2 0.2 fusion.10
  35.5 4.5 %all-to-all-done.1 = bf16[4,128,64]{1,2,0:T(8,128)(2,1)S(1)} async-done(((bf16[4,128,64]{1,2,0:T(8,128)(2,1)}), bf16[4,128,64]{1,2,0:T(8,128)(2,1)S(1)}, u32[]{:S(2)}, u32[]{:S(2)}) %all-to-all-start.1) | async-done | bytes 65568 | tf_op jit(solution)/shard_map/all_to_all | solution.py:44
  40.0 0.2 convolution_bitcast_fusion
  40.2 0.8 copy.40
  41.0 0.0 reduce-scatter.4.cloned.1.call-update
  41.0 0.2 convolution_convert_fusion.1
  41.2 0.1 copy.35
  41.3 26.9 %all-reduce = (bf16[256,64]{1,0:T(8,128)(2,1)S(1)}, bf16[256]{0:T(256)(128)(2,1)S(1)}) all-reduce(bf16[256,64]{1,0:T(8,128)(2,1)S(1)} %copy.35, bf16[256]{0:T(256)(128)(2,1)S(1)} %get-tuple-element.38), channel_id=1, replica_groups=mesh['dp'=8,'sub'=4] {'dp'}, use_global_device_ids=true, to_apply=%region_4.0 | all-reduce | flops 16640 | bytes 66560 | tf_op jit(solution)/shard_map/psum | solution.py:54
  68.3 0.1 divide_bitcast_fusion
  68.4 0.7 copy.37
  69.1 0.7 copy.36
  69.8 104.3 %reduce-scatter.4.cloned.1.call-done = f32[8,256]{1,0:T(8,128)} async-done(((f32[256,256]{1,0:T(8,128)}), f32[8,256]{1,0:T(8,128)}) %reduce-scatter.4.cloned.1.call-update) | async-done | bytes 8208
  (8 shorter events, 0.0 us)
Async XLA Ops:
  7.2 10.3 %copy-start = (bf16[128,256]{1,0:T(8,128)(2,1)S(1)}, bf16[128,256]{1,0:T(8,128)(2,1)}, u32[]{:S(2)}) copy-start(bf16[128,256]{1,0:T(8,128)(2,1)} %param.3) | copy-start | bytes 196612
  18.4 3.4 %copy-start.5 = (f32[1,256,64]{1,2,0:T(8,128)S(1)}, f32[1,256,64]{1,2,0:T(8,128)}, u32[]{:S(2)}) copy-start(f32[1,256,64]{1,2,0:T(8,128)} %param.5) | copy-start | bytes 196612
  18.4 8.2 %all-to-all-start = ((bf16[128,4,64]{0,2,1:T(8,128)(2,1)}), bf16[128,4,64]{0,2,1:T(8,128)(2,1)S(1)}, u32[]{:S(2)}, u32[]{:S(2)}) async-start(bf16[128,4,64]{0,2,1:T(8,128)(2,1)} %bitcast), calls=%async_computation | async-start | bytes 131072 | tf_op jit(solution)/shard_map/all_to_all | solution.py:12
  21.9 5.1 %copy-start.3 = (f32[1,256,64]{2,1,0:T(8,128)}, f32[1,256,64]{2,1,0:T(8,128)S(1)}, u32[]{:S(2)}) copy-start(f32[1,256,64]{2,1,0:T(8,128)S(1)} %copy.33) | copy-start | bytes 196612
  27.0 0.8 copy-start.1
  30.1 5.1 %copy-start.2 = (f32[512,256]{1,0:T(8,128)S(1)}, f32[512,256]{1,0:T(8,128)}, u32[]{:S(2)}) copy-start(f32[512,256]{1,0:T(8,128)} %copy-done.1) | copy-start | bytes 1572868
  31.9 8.1 %all-to-all-start.1 = ((bf16[4,128,64]{1,2,0:T(8,128)(2,1)}), bf16[4,128,64]{1,2,0:T(8,128)(2,1)S(1)}, u32[]{:S(2)}, u32[]{:S(2)}) async-start(bf16[4,128,64]{1,2,0:T(8,128)(2,1)} %copy.34), calls=%async_computation.1 | async-start | bytes 131072 | tf_op jit(solution)/shard_map/all_to_all | solution.py:44
  35.2 139.0 %reduce-scatter.4.cloned.1.call-start = ((), (), s32[]{:S(2)}) async-start(), calls=%async_computation.3 | async-start | bytes 270336
  41.2 27.1 %copy-start.4 = (f32[1,256,64]{2,1,0:T(8,128)S(1)}, f32[1,256,64]{2,1,0:T(8,128)}, u32[]{:S(2)}) copy-start(f32[1,256,64]{2,1,0:T(8,128)} %copy-done.3) | copy-start | bytes 196612
Sparse Core Ops, SparseCore 0:
  41.1 132.9 reduce-scatter.3
where the time goes:
time: 182 us; the launch traced here: 181 us
  waiting for transfers between devices  113 us (62%)
  blocking collectives  37.2 us (20%)
  between operations  14.2 us (8%)
  starting transfers between devices  6.74 us (4%)
  local copies, waits for them, and re-layouts  4.53 us (2%)
  Pallas kernels  2.32 us (1%)
    unnamed x2, waiting for transfers between devices  104 us
    psum x1, blocking collectives, per_device(): lax.psum(sums.astype(jnp.bfloat16), 'dp').astype(jnp.float32)  26.9 us
    all_gather x1, blocking collectives, per_device(): full_rotation = lax.all_gather(rotation, 'sub', axis=1, tiled=True)  10.2 us
    all_to_all x1, waiting for transfers between devices, per_device(): lax.all_to_all(rotated, 'sub', split_axis=1, concat_axis=0, tiled=True)  4.59 us
    all_to_all x1, waiting for transfers between devices, per_device(): lax.all_to_all(rebuilt, 'sub', split_axis=0, concat_axis=1, tiled=True)  4.53 us
  transfers between devices with their start and end apart: 3, of which 3 were waited for; matrix products, arithmetic and copies ran while one was open for 1% of the time, Pallas kernels for 0%

commit v1 on v0

v1 whole, which is shorter than its diff:
```python
import functools

import jax
import jax.numpy as jnp
from jax import lax
from jax.experimental import pallas as pl
from jax.experimental.pallas import tpu as pltpu
from jax.sharding import PartitionSpec as P

MESH = pl.DeviceIdType.MESH
F32 = jnp.float32
BF16 = jnp.bfloat16
LANES = 128
NT = (((1,), (1,)), ((), ()))
TN = (((0,), (0,)), ((), ()))


def each(count, body, start=0):
    if count - start <= 32:
        for i in range(start, count):
            body(i)
    else:
        def step(i, carry):
            body(i)
            return carry

        lax.fori_loop(start, count, step, 0)


def kernel(
    dp,
    subs,
    samples_hbm,
    rotation_hbm,
    codebook_hbm,
    recon_ref,
    new_ref,
    cross_ref,
    samples_all,
    code_own,
    rot_all,
    code_all,
    rec_part,
    rec_halves,
    pack_s,
    pack_x,
    two_s,
    two_x,
    spare,
    halves,
    final,
    local_sem,
    rot_send,
    rot_recv,
    code_send,
    code_recv,
    swap_send,
    swap_recv,
    two_s_send,
    two_s_recv,
    two_x_send,
    two_x_recv,
    new_send,
    new_recv,
):
    chips_z = dp // 2
    half = subs // 2
    group = chips_z * subs
    my_dp = lax.axis_index("dp")
    my_sub = lax.axis_index("sub")
    core = lax.rem(my_dp, 2)
    my_z = my_dp // 2
    me = my_z * subs + my_sub
    _, rows, dim = samples_all.shape
    width, codes = code_own.shape
    chunk = codes // dp
    out_rows = cross_ref.shape[0]
    home = my_sub // half == core
    home_index = lax.rem(my_sub, half)

    load_samples = pltpu.make_async_copy(samples_hbm, samples_all.at[core], local_sem.at[0])
    load_codes = pltpu.make_async_copy(codebook_hbm.at[0], code_own, local_sem.at[1])
    load_rotation = pltpu.make_async_copy(rotation_hbm, rot_all.at[home_index], local_sem.at[2])
    load_codes.start()
    load_samples.start()

    @pl.when(home)
    def _():
        load_rotation.start()

    barrier = pltpu.get_barrier_semaphore()
    everyone = dp * subs
    my_id = my_dp * subs + my_sub

    def greet(k):
        n = lax.rem(my_id + k, everyone)
        pl.semaphore_signal(
            barrier, inc=1, device_id=(n // subs, lax.rem(n, subs)), device_id_type=MESH
        )

    each(everyone, greet, 1)

    load_codes.wait()

    @pl.when(home)
    def _():
        code_t = code_own[...]
        square = jnp.sum(code_t * code_t, axis=0, keepdims=True)
        high = square.astype(BF16).astype(F32)
        middle = (square - high).astype(BF16).astype(F32)
        low = square - high - middle
        row = lax.broadcasted_iota(jnp.int32, (16, codes), 0)
        split = jnp.where(
            row == 0, high, jnp.where(row == 1, middle, jnp.where(row == 2, low, 0.0))
        )
        code_all[home_index, 0:width] = code_t.astype(BF16)
        code_all[home_index, width : width + 16] = split.astype(BF16)
        load_rotation.wait()

    load_samples.wait()
    pl.semaphore_wait(barrier, everyone - 1)

    def swap(src, dst, k):
        return pltpu.make_async_remote_copy(
            src_ref=src,
            dst_ref=dst,
            send_sem=swap_send.at[k],
            recv_sem=swap_recv.at[k],
            device_id=(2 * my_z + 1 - core, my_sub),
            device_id_type=MESH,
        )

    def gather_copy(buffer, send, recv, k, index):
        return pltpu.make_async_remote_copy(
            src_ref=buffer.at[index],
            dst_ref=buffer.at[index],
            send_sem=send.at[k],
            recv_sem=recv.at[index],
            device_id=(my_dp, lax.rem(my_sub + k, subs)),
            device_id_type=MESH,
        )

    @pl.when(home)
    def _():
        def send_gather(k):
            gather_copy(rot_all, rot_send, rot_recv, k, home_index).start()
            gather_copy(code_all, code_send, code_recv, k, home_index).start()

        each(subs, send_gather, 1)

    swap_samples = swap(samples_all.at[core], samples_all.at[core], 0)
    swap_samples.start()
    swap_samples.wait_recv()

    samples = samples_all[...].reshape(2 * rows, dim)
    ones = jnp.ones((2 * rows, LANES - width), BF16)

    def spread(src, two, send, recv, n):
        return pltpu.make_async_remote_copy(
            src_ref=src,
            dst_ref=two.at[me],
            send_sem=send.at[n],
            recv_sem=recv.at[me],
            device_id=(2 * (n // subs) + core, lax.rem(n, subs)),
            device_id_type=MESH,
        )

    def arrived(two, send, recv, n):
        return pltpu.make_async_remote_copy(
            src_ref=two.at[n],
            dst_ref=two.at[n],
            send_sem=send.at[n],
            recv_sem=recv.at[n],
            device_id=(2 * (n // subs) + core, lax.rem(n, subs)),
            device_id_type=MESH,
        )

    def chunk_of(n):
        return lax.rem(n, subs) // half * chips_z + n // subs

    def spread_s(n):
        return spread(pack_s.at[lax.rem(n, half), chunk_of(n)], two_s, two_s_send, two_s_recv, n)

    def assign(i):
        @pl.when(jnp.logical_not(jnp.logical_and(home, home_index == i)))
        def _():
            gather_copy(rot_all, rot_send, rot_recv, 1, i).wait_recv()
            gather_copy(code_all, code_send, code_recv, 1, i).wait_recv()

        rotated = lax.dot_general(samples, rot_all[i], NT, preferred_element_type=F32).astype(BF16)
        wide = rotated.astype(F32)
        row_square = jnp.sum(wide * wide, axis=1, keepdims=True)
        code_low = code_all[i, 0:width]
        code_square = jnp.sum(code_all[i, width : width + 16].astype(F32), axis=0, keepdims=True)
        inner = jnp.dot(rotated, code_low, preferred_element_type=F32)
        logits = -0.125 * (row_square - 2.0 * inner + code_square)
        powers = jnp.exp(logits - jnp.max(logits, axis=1, keepdims=True))
        weights = (powers / jnp.sum(powers, axis=1, keepdims=True)).astype(BF16)
        sums = lax.dot_general(
            weights,
            jnp.concatenate([rotated, ones], axis=1),
            TN,
            preferred_element_type=F32,
        ).reshape(dp, chunk, LANES)
        if chunk < 16:
            sums = jnp.concatenate([sums, jnp.zeros((dp, 16 - chunk, LANES), F32)], axis=1)
        pack_s[i] = sums.astype(BF16)

        def send_sums(m):
            n = half * lax.rem(me // half + m, group // half) + i
            if isinstance(m, int) and m > 0:
                spread_s(n).start()
            else:
                pl.when(n != me)(lambda: spread_s(n).start())

        each(group // half, send_sums)
        return lax.dot_general(weights, code_low, NT, preferred_element_type=F32).astype(BF16)

    recon = jnp.concatenate([assign(i) for i in range(half)], axis=1)
    rec_part[...] = recon.reshape(rec_part.shape)
    swap_recon = swap(rec_part.at[1 - core], rec_halves.at[core], 1)
    swap_recon.start()

    cross = lax.dot_general(samples, recon, TN, preferred_element_type=F32)
    cross = cross.reshape(chips_z, 2, subs, out_rows, dim // 2)
    pack_x[...] = (
        jnp.concatenate(
            [cross[:, c, ..., j : j + LANES] for c in range(2) for j in range(0, dim // 2, LANES)],
            axis=2,
        )
        .astype(BF16)
        .reshape(pack_x.shape)
    )

    def spread_x(k):
        n = lax.rem(me + k, group)
        return spread(pack_x.at[n], two_x, two_x_send, two_x_recv, n)

    each(group, lambda k: spread_x(k).start(), 1)
    rec_halves[core] = rec_part[core]
    two_s[me] = pack_s[lax.rem(me, half), chunk_of(me)]
    two_x[me] = pack_x[me]

    def wait_s(k):
        arrived(two_s, two_s_send, two_s_recv, lax.rem(me + k, group)).wait_recv()

    each(group, wait_s, 1)
    mine = chunk_of(me)
    final[mine] = jnp.sum(two_s[...].astype(F32), axis=0).astype(BF16)
    owned = core * half + home_index

    def share(t):
        return pltpu.make_async_remote_copy(
            src_ref=final.at[mine],
            dst_ref=spare.at[mine],
            send_sem=new_send.at[t],
            recv_sem=new_recv.at[mine],
            device_id=(lax.rem(my_dp + t, dp), owned),
            device_id_type=MESH,
        )

    each(dp, lambda t: share(t).start(), 1)

    @pl.when(home)
    def _():
        spare[mine] = final[mine]

    @pl.when(jnp.logical_not(home))
    def _():
        share(0).start()

    def wait_x(k):
        arrived(two_x, two_x_send, two_x_recv, lax.rem(me + k, group)).wait_recv()

    each(group, wait_x, 1)
    total_x = jnp.sum(two_x[...].astype(F32), axis=0)
    tall = total_x.shape[0] // 2
    final_x = total_x.reshape(2, tall, LANES)
    halves[2:4] = final_x
    swap_x = swap(halves.at[3 - core], halves.at[core], 2)
    swap_x.start()
    halves[core] = halves[2 + core]
    swap_recon.wait_recv()
    for c in range(2):
        recon_ref[:, c * (dim // 2) : (c + 1) * (dim // 2)] = rec_halves[c]

    def received(t):
        j = lax.rem(mine + t, dp)
        return pltpu.make_async_remote_copy(
            src_ref=spare.at[j],
            dst_ref=spare.at[j],
            send_sem=new_send.at[0],
            recv_sem=new_recv.at[j],
            device_id=(my_dp, owned),
            device_id_type=MESH,
        )

    swap_x.wait_recv()
    for c in range(2):
        for j in range(dim // 2 // LANES):
            at = c * (dim // 2) + j * LANES
            cross_ref[:, at : at + LANES] = halves[c, j * out_rows : (j + 1) * out_rows]

    each(dp, lambda t: received(t).wait_recv(), 1)

    @pl.when(jnp.logical_not(home))
    def _():
        received(0).wait_recv()

    totals = spare[...].astype(F32)[:, :chunk].reshape(codes, LANES).T
    new_ref[0] = (totals[:width] + code_own[...]) / (totals[width : 2 * width] + 1.0)

    @pl.when(home)
    def _():
        def finish(k):
            gather_copy(rot_all, rot_send, rot_recv, k, home_index).wait_send()
            gather_copy(code_all, code_send, code_recv, k, home_index).wait_send()

        each(subs, finish, 1)

    @pl.when(jnp.logical_not(home))
    def _():
        share(0).wait_send()

    swap_samples.wait_send()
    swap_recon.wait_send()
    swap_x.wait_send()
    each(group, lambda k: spread_s(lax.rem(me + k, group)).wait_send(), 1)
    each(group, lambda k: spread_x(k).wait_send(), 1)
    each(dp, lambda t: share(t).wait_send(), 1)


def write_kernel(recon_ref, new_ref, cross_ref, recon_out, new_out, cross_out, sems):
    pairs = ((recon_ref, recon_out), (new_ref, new_out), (cross_ref, cross_out))
    copies = [pltpu.make_async_copy(s, d, sems.at[i]) for i, (s, d) in enumerate(pairs)]
    for copy in copies:
        copy.start()
    for copy in copies:
        copy.wait()


def per_device(dp, subs, samples, rotation, codebook):
    rows, dim = samples.shape
    codes, width = codebook.shape[1:]
    half = subs // 2
    group = dp // 2 * subs
    chunk = max(16, codes // dp)
    out_rows = dim // (dp * subs)
    tile = out_rows * dim // LANES
    dma = pltpu.SemaphoreType.DMA
    vmem = pl.BlockSpec(memory_space=pltpu.VMEM)
    hbm = pl.BlockSpec(memory_space=pltpu.HBM)
    shapes = (
        jax.ShapeDtypeStruct((rows, dim), BF16),
        jax.ShapeDtypeStruct((1, width, codes), F32),
        jax.ShapeDtypeStruct((out_rows, dim), F32),
    )
    parts = pl.pallas_call(
        functools.partial(kernel, dp, subs),
        out_shape=shapes,
        in_specs=[hbm] * 3,
        out_specs=(vmem,) * 3,
        scratch_shapes=[
            pltpu.VMEM((2, rows, dim), BF16),
            pltpu.VMEM((width, codes), F32),
            pltpu.VMEM((half, width, dim), BF16),
            pltpu.VMEM((half, width + 16, codes), BF16),
            pltpu.VMEM((2, rows, dim // 2), BF16),
            pltpu.VMEM((2, rows, dim // 2), BF16),
            pltpu.VMEM((half, dp, chunk, LANES), BF16),
            pltpu.VMEM((group, tile, LANES), BF16),
            pltpu.VMEM((group, chunk, LANES), BF16),
            pltpu.VMEM((group, tile, LANES), BF16),
            pltpu.VMEM((dp, chunk, LANES), BF16),
            pltpu.VMEM((4, tile // 2, LANES), F32),
            pltpu.VMEM((dp, chunk, LANES), BF16),
            dma((3,)),
            dma((subs,)),
            dma((half,)),
            dma((subs,)),
            dma((half,)),
            dma((3,)),
            dma((3,)),
            dma((group,)),
            dma((group,)),
            dma((group,)),
            dma((group,)),
            dma((dp,)),
            dma((dp,)),
        ],
        compiler_params=pltpu.CompilerParams(
            collective_id=0, has_side_effects=True, vmem_limit_bytes=40 * 1024 * 1024
        ),
    )(samples, rotation.T, codebook.swapaxes(1, 2))
    recon, new_codes, cross = pl.pallas_call(
        write_kernel,
        out_shape=shapes,
        in_specs=[vmem] * 3,
        out_specs=(hbm,) * 3,
        scratch_shapes=[dma((3,))],
    )(*parts)
    return recon, new_codes.swapaxes(1, 2), cross


def solution(mesh):
    in_specs = (P(("dp", "sub"), None), P(None, "sub"), P("sub", None, None))
    out_specs = (P(("dp", "sub"), None), P("sub", None, None), P(("dp", "sub"), None))
    return jax.shard_map(
        functools.partial(per_device, mesh.shape["dp"], mesh.shape["sub"]),
        mesh=mesh,
        in_specs=in_specs,
        out_specs=out_specs,
        check_vma=False,
    )
```

time: 182 us -> 28.9 us (0.16)
  waiting for transfers between devices: 113 us -> 0 us
  blocking collectives: 37.2 us -> 0 us
  Pallas kernels: 2.32 us -> 23.6 us
  between operations: 14.2 us -> 0.66 us
  starting transfers between devices: 6.74 us -> 0 us
    unnamed x2 -> x0, waiting for transfers between devices: 104 us -> none
    psum x1 -> x0, blocking collectives: 26.9 us -> none  [per_device(): lax.psum(sums.astype(jnp.bfloat16), 'dp').astype(jnp.float32)]
    pallas_call x0 -> x2, Pallas kernels: none -> 23.6 us  [the longest x1 22.1 us: per_device(): pl.pallas_call(functools.partial(kernel, dp, subs), out_shape=shapes, in_...]
    all_gather x1 -> x0, blocking collectives: 10.2 us -> none  [per_device(): full_rotation = lax.all_gather(rotation, 'sub', axis=1, tiled=True)]
    all_to_all x2 -> x0, waiting for transfers between devices: 9.12 us -> none  [the longest x1 4.59 us: per_device(): lax.all_to_all(rotated, 'sub', split_axis=1, concat_axis=0, tiled=True)]
    all_to_all x2 -> x0, starting transfers between devices: 6.7 us -> none  [the longest x1 3.42 us: per_device(): lax.all_to_all(rotated, 'sub', split_axis=1, concat_axis=0, tiled=True)]
    unnamed x1 -> x0, Pallas kernels: 2.32 us -> none
    unnamed x16 -> x12, local copies, waits for them, and re-layouts: 2.95 us -> 4.25 us
  transfers between devices with their start and end apart: 3 -> 0, of which waited for: 3 -> 0; matrix products, arithmetic and copies ran while one was open for 1% -> 0% of each run, Pallas kernels for 0% -> 0%
where the time goes in v1:
time: 28.9 us; the launch traced here: 28.5 us
  Pallas kernels  23.6 us (82%)
  local copies, waits for them, and re-layouts  4.25 us (15%)
  between operations  0.66 us (2%)
    pallas_call x1, Pallas kernels, per_device(): pl.pallas_call(functools.partial(kernel, dp, subs), out_shape=shapes, in_...  22.1 us
    unnamed x12, local copies, waits for them, and re-layouts  4.25 us
    pallas_call x1, Pallas kernels, per_device(): pl.pallas_call(write_kernel, out_shape=shapes, in_specs=[vmem] * 3, out_s...  1.55 us

profile of v1, /device:TPU:0, one launch (start us, length us, event | category | flops | bytes accessed | tf_op | source)
XLA Modules:
  0.0 28.5 jit_solution(7704661050845769500)
XLA Ops:
  0.6 0.0 copy-start
  0.6 0.8 %copy-done = bf16[128,256]{1,0:T(8,128)(2,1)S(1)} copy-done((bf16[128,256]{1,0:T(8,128)(2,1)S(1)}, bf16[128,256]{1,0:T(8,128)(2,1)}, u32[]{:S(2)}) %copy-start) | copy-done | bytes 65560
  1.5 0.0 copy-start.1
  1.5 0.8 %copy-done.1 = f32[1,256,64]{1,2,0:T(8,128)S(1)} copy-done((f32[1,256,64]{1,2,0:T(8,128)S(1)}, f32[1,256,64]{1,2,0:T(8,128)}, u32[]{:S(2)}) %copy-start.1) | copy-done | bytes 65560
  2.3 0.0 copy-start.4
  2.3 0.8 %copy-done.4 = bf16[256,64]{0,1:T(8,128)(2,1)S(1)} copy-done((bf16[256,64]{0,1:T(8,128)(2,1)S(1)}, bf16[256,64]{0,1:T(8,128)(2,1)}, u32[]{:S(2)}) %copy-start.4) | copy-done | bytes 32792
  3.1 22.1 %shard_map.58 = (bf16[128,256]{1,0:T(8,128)(2,1)S(1)}, f32[1,64,256]{2,1,0:T(8,128)S(1)}, f32[8,256]{1,0:T(8,128)S(1)}) custom-call(bf16[128,256]{1,0:T(8,128)(2,1)S(1)} %copy-done, bf16[64,256]{1,0:T(8,128)(2,1)S(1)} %bitcast.4, f32[1,64,256]{2,1,0:T(8,128)S(1)} %bitcast.3), custom_call_target="tpu_custom_call" | custom-call | tf_op jit(solution)/shard_map/pallas_call | solution.py:358
  25.2 0.0 copy-start.2
  25.2 0.6 %copy-done.2 = bf16[128,256]{1,0:T(8,128)(2,1)} copy-done((bf16[128,256]{1,0:T(8,128)(2,1)}, bf16[128,256]{1,0:T(8,128)(2,1)S(1)}, u32[]{:S(2)}) %copy-start.2) | copy-done | bytes 65560
  25.8 0.0 copy-start.3
  25.8 0.6 %copy-done.3 = f32[1,64,256]{2,1,0:T(8,128)} copy-done((f32[1,64,256]{2,1,0:T(8,128)}, f32[1,64,256]{2,1,0:T(8,128)S(1)}, u32[]{:S(2)}) %copy-start.3) | copy-done | bytes 65560
  26.4 0.0 copy-start.5
  26.4 0.6 %copy-done.5 = f32[8,256]{1,0:T(8,128)} copy-done((f32[8,256]{1,0:T(8,128)}, f32[8,256]{1,0:T(8,128)S(1)}, u32[]{:S(2)}) %copy-start.5) | copy-done | bytes 8216
  27.0 1.5 %shard_map.59 = (bf16[128,256]{1,0:T(8,128)(2,1)}, f32[1,64,256]{2,1,0:T(8,128)}, f32[8,256]{1,0:T(8,128)}) custom-call(bf16[128,256]{1,0:T(8,128)(2,1)} %copy-done.2, f32[1,64,256]{2,1,0:T(8,128)} %copy-done.3, f32[8,256]{1,0:T(8,128)} %copy-done.5), custom_call_target="tpu_custom_call" | custom-call | tf_op jit(solution)/shard_map/pallas_call | solution.py:395
Async XLA Ops:
  0.6 0.8 %copy-start = (bf16[128,256]{1,0:T(8,128)(2,1)S(1)}, bf16[128,256]{1,0:T(8,128)(2,1)}, u32[]{:S(2)}) copy-start(bf16[128,256]{1,0:T(8,128)(2,1)} %samples_hbm.1) | copy-start | bytes 196612
  1.5 0.8 %copy-start.1 = (f32[1,256,64]{1,2,0:T(8,128)S(1)}, f32[1,256,64]{1,2,0:T(8,128)}, u32[]{:S(2)}) copy-start(f32[1,256,64]{1,2,0:T(8,128)} %param.5) | copy-start | bytes 196612
  2.3 0.8 %copy-start.4 = (bf16[256,64]{0,1:T(8,128)(2,1)S(1)}, bf16[256,64]{0,1:T(8,128)(2,1)}, u32[]{:S(2)}) copy-start(bf16[256,64]{0,1:T(8,128)(2,1)} %param.4) | copy-start | bytes 98308
  25.2 0.6 %copy-start.2 = (bf16[128,256]{1,0:T(8,128)(2,1)}, bf16[128,256]{1,0:T(8,128)(2,1)S(1)}, u32[]{:S(2)}) copy-start(bf16[128,256]{1,0:T(8,128)(2,1)S(1)} %get-tuple-element.9.recon_ref) | copy-start | bytes 196612
  25.8 0.6 %copy-start.3 = (f32[1,64,256]{2,1,0:T(8,128)}, f32[1,64,256]{2,1,0:T(8,128)S(1)}, u32[]{:S(2)}) copy-start(f32[1,64,256]{2,1,0:T(8,128)S(1)} %get-tuple-element.10.new_ref) | copy-start | bytes 196612
  26.4 0.6 %copy-start.5 = (f32[8,256]{1,0:T(8,128)}, f32[8,256]{1,0:T(8,128)S(1)}, u32[]{:S(2)}) copy-start(f32[8,256]{1,0:T(8,128)S(1)} %get-tuple-element.11.cross_ref) | copy-start | bytes 24580

commit v2 on v1

--- a/solution.py
+++ b/solution.py
@@ -391,13 +391,14 @@
         compiler_params=pltpu.CompilerParams(
             collective_id=0, has_side_effects=True, vmem_limit_bytes=40 * 1024 * 1024
         ),
-    )(samples, rotation.T, codebook.swapaxes(1, 2))
+    )(*(pltpu.with_memory_space_constraint(x, pltpu.HBM) for x in (samples, rotation.T, codebook.swapaxes(1, 2))))
     recon, new_codes, cross = pl.pallas_call(
         write_kernel,
         out_shape=shapes,
         in_specs=[vmem] * 3,
         out_specs=(hbm,) * 3,
         scratch_shapes=[dma((3,))],
+        compiler_params=pltpu.CompilerParams(vmem_limit_bytes=4 * 1024 * 1024),
     )(*parts)
     return recon, new_codes.swapaxes(1, 2), cross
 

time: 28.9 us -> 23.5 us (0.81)
  local copies, waits for them, and re-layouts: 4.25 us -> 0 us
  Pallas kernels: 23.6 us -> 22.7 us
    unnamed x12 -> x0, local copies, waits for them, and re-layouts: 4.25 us -> none
    pallas_call x1, Pallas kernels: 1.55 us -> 0.68 us  [per_device(): pl.pallas_call(write_kernel, out_shape=shapes, in_specs=[vmem] * 3, out_s...]
where the time goes in v2:
time: 23.5 us; the launch traced here: 23.3 us
  Pallas kernels  22.7 us (97%)
  between operations  0.64 us (3%)
    pallas_call x1, Pallas kernels, per_device(): pl.pallas_call(functools.partial(kernel, dp, subs), out_shape=shapes, in_...  22 us
    pallas_call x1, Pallas kernels, per_device(): pl.pallas_call(write_kernel, out_shape=shapes, in_specs=[vmem] * 3, out_s...  0.68 us

profile of v2, /device:TPU:0, one launch (start us, length us, event | category | flops | bytes accessed | tf_op | source)
XLA Modules:
  0.0 23.3 jit_solution(2041911057879954373)
XLA Ops:
  0.6 22.0 %shard_map.58 = (bf16[128,256]{1,0:T(8,128)(2,1)S(1)}, f32[1,64,256]{2,1,0:T(8,128)S(1)}, f32[8,256]{1,0:T(8,128)S(1)}) custom-call(bf16[128,256]{1,0:T(8,128)(2,1)} %samples_hbm.1, bf16[64,256]{1,0:T(8,128)(2,1)} %bitcast.4, f32[1,64,256]{2,1,0:T(8,128)} %bitcast.3), custom_call_target="tpu_custom_call" | custom-call | tf_op jit(solution)/shard_map/pallas_call | solution.py:358
  22.6 0.7 %shard_map.59 = (bf16[128,256]{1,0:T(8,128)(2,1)}, f32[1,64,256]{2,1,0:T(8,128)}, f32[8,256]{1,0:T(8,128)}) custom-call(bf16[128,256]{1,0:T(8,128)(2,1)S(1)} %get-tuple-element.9.recon_ref, f32[1,64,256]{2,1,0:T(8,128)S(1)} %get-tuple-element.10.new_ref, f32[8,256]{1,0:T(8,128)S(1)} %get-tuple-element.11.cross_ref), custom_call_target="tpu_custom_call" | custom-call | tf_op jit(solution)/shard_map/pallas_call | solution.py:395

commit v3 on v2

v3 whole, which is shorter than its diff:
```python
import functools

import jax
import jax.numpy as jnp
from jax import lax
from jax.experimental import pallas as pl
from jax.experimental.pallas import tpu as pltpu
from jax.sharding import PartitionSpec as P

MESH = pl.DeviceIdType.MESH
F32 = jnp.float32
BF16 = jnp.bfloat16
LANES = 128
NT = (((1,), (1,)), ((), ()))
TN = (((0,), (0,)), ((), ()))


def each(count, body, start=0):
    if count - start <= 32:
        for i in range(start, count):
            body(i)
    else:
        def step(i, carry):
            body(i)
            return carry

        lax.fori_loop(start, count, step, 0)


def kernel(
    dp,
    subs,
    samples_hbm,
    rotation_hbm,
    codebook_hbm,
    recon_ref,
    new_ref,
    cross_ref,
    samples_all,
    samples_t,
    code_own,
    rot_all,
    code_all,
    rec_part,
    rec_halves,
    pack_s,
    pack_x,
    two_s,
    two_x,
    count_out,
    count_in,
    own_total,
    totals,
    halves,
    local_sem,
    gather_send,
    rot_recv,
    code_recv,
    swap_send,
    swap_recv,
    many_send,
    many_recv,
):
    chips_z = dp // 2
    half = subs // 2
    group = chips_z * subs
    my_dp = lax.axis_index("dp")
    my_sub = lax.axis_index("sub")
    core = lax.rem(my_dp, 2)
    my_z = my_dp // 2
    my_part = my_sub // half
    me = my_z * subs + my_sub
    _, rows, dim = samples_all.shape
    width, codes = code_own.shape
    chunk = width // dp
    out_rows = cross_ref.shape[0]
    home = my_part == core
    home_index = my_sub - my_part * half
    mine = my_part * chips_z + my_z
    owned = core * half + home_index

    def wrap(index, count):
        return jnp.where(index >= count, index - count, index)

    load_samples = pltpu.make_async_copy(samples_hbm, samples_all.at[core], local_sem.at[0])
    load_codes = pltpu.make_async_copy(codebook_hbm.at[0], code_own, local_sem.at[1])
    load_rotation = pltpu.make_async_copy(rotation_hbm, rot_all.at[home_index], local_sem.at[2])

    barrier = pltpu.get_barrier_semaphore()

    def greet(k):
        d = wrap(my_dp + k, dp)
        for j in range(subs):
            if isinstance(k, int) and k == 0 and j == 0:
                continue
            pl.semaphore_signal(
                barrier, inc=1, device_id=(d, wrap(my_sub + j, subs)), device_id_type=MESH
            )

    each(dp, greet)
    load_codes.start()
    load_samples.start()

    @pl.when(home)
    def _():
        load_rotation.start()

    load_codes.wait()

    @pl.when(home)
    def _():
        code_t = code_own[...]
        square = -0.5 * jnp.sum(code_t * code_t, axis=0, keepdims=True)
        high = square.astype(BF16).astype(F32)
        middle = (square - high).astype(BF16).astype(F32)
        low = square - high - middle
        row = lax.broadcasted_iota(jnp.int32, (16, codes), 0)
        split = jnp.where(
            row == 0, high, jnp.where(row == 1, middle, jnp.where(row == 2, low, 0.0))
        )
        code_all[home_index, 0:width] = code_t.astype(BF16)
        code_all[home_index, width : width + 16] = split.astype(BF16)
        load_rotation.wait()

    load_samples.wait()
    pl.semaphore_wait(barrier, dp * subs - 1)

    def remote(src, dst, send, recv, device):
        return pltpu.make_async_remote_copy(
            src_ref=src,
            dst_ref=dst,
            send_sem=send,
            recv_sem=recv,
            device_id=device,
            device_id_type=MESH,
        )

    partner = (my_dp + 1 - 2 * core, my_sub)

    def swap(src, dst, k):
        return remote(src, dst, swap_send.at[k], swap_recv.at[k], partner)

    def rot_copy(index, k, device):
        slot = rot_all.at[index]
        return remote(slot, slot, gather_send.at[k], rot_recv.at[index], device)

    def code_copy(index, k, device):
        slot = code_all.at[index]
        return remote(slot, slot, gather_send.at[subs + k], code_recv.at[index], device)

    def gather_peer(k):
        return (my_dp, wrap(my_sub + k, subs))

    swap_samples = swap(samples_all.at[core], samples_all.at[core], 0)
    swap_samples.start()

    @pl.when(home)
    def _():
        for k in range(1, subs):
            rot_copy(home_index, k, gather_peer(k)).start()
        for k in range(1, subs):
            code_copy(home_index, k, gather_peer(k)).start()

    swap_samples.wait_recv()
    samples_t[...] = samples_all[...].reshape(2 * rows, dim).astype(F32).T.astype(BF16)

    for i in range(half):
        @pl.when(jnp.logical_not(jnp.logical_and(home, home_index == i)))
        def _():
            rot_copy(i, 1, partner).wait_recv()
            code_copy(i, 1, partner).wait_recv()

    rotated_all = jnp.dot(
        rot_all[...].reshape(half * width, dim), samples_t[...], preferred_element_type=F32
    ).astype(BF16)
    ones = jnp.ones((16, 2 * rows), BF16)
    recon = []
    for i in range(half):
        rotated = rotated_all[i * width : (i + 1) * width]
        wide = rotated.astype(F32)
        row_square = jnp.sum(wide * wide, axis=0, keepdims=True)
        tall = jnp.concatenate([rotated, ones], axis=0)
        inner = lax.dot_general(code_all[i], tall, TN, preferred_element_type=F32)
        logits = -0.125 * (row_square - 2.0 * inner)
        powers = jnp.exp(logits - jnp.max(logits, axis=0, keepdims=True))
        weights = (powers * (1.0 / jnp.sum(powers, axis=0, keepdims=True))).astype(BF16)
        sums = lax.dot_general(tall, weights, NT, preferred_element_type=F32)
        count_out[i] = sums[width : width + 1]
        pieces = sums[:width].reshape(dp, chunk, codes)
        pieces = jnp.concatenate(
            [pieces[..., j : j + LANES] for j in range(0, codes, LANES)], axis=1
        )
        fill = pack_s.shape[2] - pieces.shape[1]
        if fill:
            pieces = jnp.concatenate([pieces, jnp.zeros((dp, fill, LANES), F32)], axis=1)
        pack_s[i] = pieces.astype(BF16)
        recon.append(
            jnp.dot(code_all[i, 0:width], weights, preferred_element_type=F32).astype(BF16)
        )

    def each_peer(body):
        def plane(dz):
            z = wrap(my_z + dz, chips_z)
            for p in range(2):
                part = wrap(my_part + p, 2)
                for i in range(half):
                    if isinstance(dz, int) and (dz > 0 or p > 0):
                        body(z, part, i)
                    else:
                        other = jnp.logical_or(i != home_index, jnp.logical_or(dz > 0, p > 0))
                        pl.when(other)(functools.partial(body, z, part, i))

        each(chips_z, plane)

    def send_s(z, part, i):
        remote(
            pack_s.at[i, part * chips_z + z],
            two_s.at[me],
            many_send.at[0],
            many_recv.at[0],
            (2 * z + core, part * half + i),
        ).start()

    def send_x(z, part, i):
        sub = part * half + i
        remote(
            pack_x.at[z * subs + sub],
            two_x.at[me],
            many_send.at[1],
            many_recv.at[1],
            (2 * z + core, sub),
        ).start()

    each_peer(send_s)

    recon = jnp.concatenate(recon, axis=0)
    cross = lax.dot_general(samples_t[...], recon, NT, preferred_element_type=F32)
    cross = cross.reshape(chips_z, 2, subs, out_rows, dim // 2)
    pack_x[...] = (
        jnp.concatenate(
            [cross[:, c, ..., j : j + LANES] for c in range(2) for j in range(0, dim // 2, LANES)],
            axis=2,
        )
        .astype(BF16)
        .reshape(pack_x.shape)
    )
    each_peer(send_x)

    def send_count(t, i):
        return remote(
            count_out.at[i],
            count_in.at[me],
            many_send.at[2],
            many_recv.at[2],
            (wrap(my_dp + t, dp), core * half + i),
        )

    def send_counts(t):
        for i in range(half):
            if isinstance(t, int) and t > 0:
                send_count(t, i).start()
            else:
                self = jnp.logical_and(t == 0, jnp.logical_and(home, home_index == i))
                pl.when(jnp.logical_not(self))(lambda: send_count(t, i).start())

    each(dp, send_counts)

    @pl.when(home)
    def _():
        count_in[me] = count_out[home_index]

    rec_part[...] = recon.astype(F32).T.astype(BF16).reshape(rec_part.shape)
    swap_recon = swap(rec_part.at[1 - core], rec_halves.at[core], 1)
    swap_recon.start()
    rec_halves[core] = rec_part[core]
    two_s[me] = pack_s[home_index, mine]
    two_x[me] = pack_x[me]

    def wait_recv(buffer, count, k):
        part = buffer.at[pl.ds(0, count)]
        remote(part, part, many_send.at[k], many_recv.at[k], partner).wait_recv()

    def wait_send(buffer, count, k):
        part = buffer.at[pl.ds(0, count)]
        remote(part, part, many_send.at[k], many_recv.at[k], partner).wait_send()

    wait_recv(two_s, group - 1, 0)
    own_total[...] = jnp.sum(two_s[...].astype(F32), axis=0).astype(BF16)

    def share(t):
        return remote(
            own_total, totals.at[mine], many_send.at[3], many_recv.at[3], (wrap(my_dp + t, dp), owned)
        )

    each(dp, lambda t: share(t).start(), 1)

    @pl.when(home)
    def _():
        totals[mine] = own_total[...]

    @pl.when(jnp.logical_not(home))
    def _():
        share(0).start()

    wait_recv(two_x, group - 1, 1)
    total_x = jnp.sum(two_x[...].astype(F32), axis=0)
    halves[2:4] = total_x.reshape(2, total_x.shape[0] // 2, LANES)
    swap_x = swap(halves.at[3 - core], halves.at[core], 2)
    swap_x.start()
    halves[core] = halves[2 + core]
    swap_recon.wait_recv()
    for c in range(2):
        recon_ref[:, c * (dim // 2) : (c + 1) * (dim // 2)] = rec_halves[c]
    swap_x.wait_recv()
    for c in range(2):
        for j in range(dim // 2 // LANES):
            at = c * (dim // 2) + j * LANES
            cross_ref[:, at : at + LANES] = halves[c, j * out_rows : (j + 1) * out_rows]

    @pl.when(home)
    def _():
        wait_recv(count_in, group - 1, 2)
        wait_recv(totals, dp - 1, 3)
        wait_send(count_in, group - 1, 2)
        wait_send(totals, dp - 1, 3)
        for k in range(1, subs):
            rot_copy(home_index, k, partner).wait_send()
            code_copy(home_index, k, partner).wait_send()

    @pl.when(jnp.logical_not(home))
    def _():
        wait_recv(count_in, group, 2)
        wait_recv(totals, dp, 3)
        wait_send(count_in, group, 2)
        wait_send(totals, dp, 3)

    counts = jnp.sum(count_in[...], axis=0) + 1.0
    all_totals = totals[...].astype(F32)
    for j in range(codes // LANES):
        lanes = slice(j * LANES, (j + 1) * LANES)
        sums = all_totals[:, j * chunk : (j + 1) * chunk].reshape(width, LANES)
        new_ref[0, :, lanes] = (sums + code_own[:, lanes]) / counts[:, lanes]

    swap_samples.wait_send()
    swap_recon.wait_send()
    swap_x.wait_send()
    wait_send(two_s, group - 1, 0)
    wait_send(two_x, group - 1, 1)


def write_kernel(recon_ref, new_ref, cross_ref, recon_out, new_out, cross_out, sems):
    pairs = ((recon_ref, recon_out), (new_ref, new_out), (cross_ref, cross_out))
    copies = [pltpu.make_async_copy(s, d, sems.at[i]) for i, (s, d) in enumerate(pairs)]
    for copy in copies:
        copy.start()
    for copy in copies:
        copy.wait()


def per_device(dp, subs, samples, rotation, codebook):
    rows, dim = samples.shape
    codes, width = codebook.shape[1:]
    half = subs // 2
    group = dp // 2 * subs
    chunk = max(16, width * codes // (dp * LANES))
    out_rows = dim // (dp * subs)
    tile = out_rows * dim // LANES
    dma = pltpu.SemaphoreType.DMA
    vmem = pl.BlockSpec(memory_space=pltpu.VMEM)
    hbm = pl.BlockSpec(memory_space=pltpu.HBM)
    shapes = (
        jax.ShapeDtypeStruct((rows, dim), BF16),
        jax.ShapeDtypeStruct((1, width, codes), F32),
        jax.ShapeDtypeStruct((out_rows, dim), F32),
    )
    parts = pl.pallas_call(
        functools.partial(kernel, dp, subs),
        out_shape=shapes,
        in_specs=[hbm] * 3,
        out_specs=(vmem,) * 3,
        scratch_shapes=[
            pltpu.VMEM((2, rows, dim), BF16),
            pltpu.VMEM((dim, 2 * rows), BF16),
            pltpu.VMEM((width, codes), F32),
            pltpu.VMEM((half, width, dim), BF16),
            pltpu.VMEM((half, width + 16, codes), BF16),
            pltpu.VMEM((2, rows, dim // 2), BF16),
            pltpu.VMEM((2, rows, dim // 2), BF16),
            pltpu.VMEM((half, dp, chunk, LANES), BF16),
            pltpu.VMEM((group, tile, LANES), BF16),
            pltpu.VMEM((group, chunk, LANES), BF16),
            pltpu.VMEM((group, tile, LANES), BF16),
            pltpu.VMEM((half, 1, codes), F32),
            pltpu.VMEM((group, 1, codes), F32),
            pltpu.VMEM((chunk, LANES), BF16),
            pltpu.VMEM((dp, chunk, LANES), BF16),
            pltpu.VMEM((4, tile // 2, LANES), F32),
            dma((3,)),
            dma((2 * subs,)),
            dma((half,)),
            dma((half,)),
            dma((3,)),
            dma((3,)),
            dma((4,)),
            dma((4,)),
        ],
        compiler_params=pltpu.CompilerParams(
            collective_id=0, has_side_effects=True, vmem_limit_bytes=40 * 1024 * 1024
        ),
    )(
        *(
            pltpu.with_memory_space_constraint(x, pltpu.HBM)
            for x in (samples, rotation.T, codebook.swapaxes(1, 2))
        )
    )
    recon, new_codes, cross = pl.pallas_call(
        write_kernel,
        out_shape=shapes,
        in_specs=[vmem] * 3,
        out_specs=(hbm,) * 3,
        scratch_shapes=[dma((3,))],
        compiler_params=pltpu.CompilerParams(vmem_limit_bytes=4 * 1024 * 1024),
    )(*parts)
    return recon, new_codes.swapaxes(1, 2), cross


def solution(mesh):
    in_specs = (P(("dp", "sub"), None), P(None, "sub"), P("sub", None, None))
    out_specs = (P(("dp", "sub"), None), P("sub", None, None), P(("dp", "sub"), None))
    return jax.shard_map(
        functools.partial(per_device, mesh.shape["dp"], mesh.shape["sub"]),
        mesh=mesh,
        in_specs=in_specs,
        out_specs=out_specs,
        check_vma=False,
    )
```

time: 23.5 us -> 22.8 us (0.970)
  Pallas kernels: 22.7 us -> 22 us
    pallas_call x1, Pallas kernels: 22 us -> 21.3 us  [per_device(): pl.pallas_call(functools.partial(kernel, dp, subs), out_shape=shapes, in_...]
where the time goes in v3:
time: 22.8 us; the launch traced here: 22.6 us
  Pallas kernels  22 us (96%)
  between operations  0.64 us (3%)
    pallas_call x1, Pallas kernels, per_device(): pl.pallas_call(functools.partial(kernel, dp, subs), out_shape=shapes, in_...  21.3 us
    pallas_call x1, Pallas kernels, per_device(): pl.pallas_call(write_kernel, out_shape=shapes, in_specs=[vmem] * 3, out_s...  0.68 us

profile of v3, /device:TPU:0, one launch (start us, length us, event | category | flops | bytes accessed | tf_op | source)
XLA Modules:
  0.0 22.6 jit_solution(18269977735762496551)
XLA Ops:
  0.6 21.3 %shard_map.58 = (bf16[128,256]{1,0:T(8,128)(2,1)S(1)}, f32[1,64,256]{2,1,0:T(8,128)S(1)}, f32[8,256]{1,0:T(8,128)S(1)}) custom-call(bf16[128,256]{1,0:T(8,128)(2,1)} %samples_hbm.1, bf16[64,256]{1,0:T(8,128)(2,1)} %bitcast.4, f32[1,64,256]{2,1,0:T(8,128)} %bitcast.3), custom_call_target="tpu_custom_call" | custom-call | tf_op jit(solution)/shard_map/pallas_call | solution.py:376
  22.0 0.7 %shard_map.59 = (bf16[128,256]{1,0:T(8,128)(2,1)}, f32[1,64,256]{2,1,0:T(8,128)}, f32[8,256]{1,0:T(8,128)}) custom-call(bf16[128,256]{1,0:T(8,128)(2,1)S(1)} %get-tuple-element.9.recon_ref, f32[1,64,256]{2,1,0:T(8,128)S(1)} %get-tuple-element.10.new_ref, f32[8,256]{1,0:T(8,128)S(1)} %get-tuple-element.11.cross_ref), custom_call_target="tpu_custom_call" | custom-call | tf_op jit(solution)/shard_map/pallas_call | solution.py:416

commit v4 on v0

v4 whole, which is shorter than its diff:
```python
import functools

import jax
import jax.numpy as jnp
from jax import lax
from jax.experimental import pallas as pl
from jax.experimental.pallas import tpu as pltpu
from jax.sharding import PartitionSpec as P

MESH = pl.DeviceIdType.MESH
F32 = jnp.float32
BF16 = jnp.bfloat16
LANES = 128
NT = (((1,), (1,)), ((), ()))
TN = (((0,), (0,)), ((), ()))


def kernel(
    dp,
    subs,
    samples_hbm,
    rotation_hbm,
    codebook_hbm,
    recon_ref,
    new_ref,
    cross_ref,
    blocks,
    rotation,
    code_own,
    code_tall,
    rec_out,
    rec_in,
    pack_s,
    pack_x,
    two_s,
    two_x,
    count_out,
    count_in,
    own_total,
    totals,
    cross_out,
    cross_in,
    local_sem,
    block_send,
    block_recv,
    many_send,
    many_recv,
):
    half = subs // 2
    my_dp = lax.axis_index("dp")
    my_sub = lax.axis_index("sub")
    my_part = my_sub // half
    my_place = my_sub - my_part * half
    _, rows, dim = blocks.shape
    width, codes = code_own.shape
    chunk = width // dp
    out_rows = cross_ref.shape[0]

    def wrap(index, count):
        return jnp.where(index >= count, index - count, index)

    steps = [(p, q) for p in range(2) for q in range(half)]

    def towards(k):
        p, q = steps[k]
        return wrap(my_part + p, 2) * half + wrap(my_place + q, half)

    def origin(k):
        p, q = steps[k]
        return wrap(my_part + 2 - p, 2) * half + wrap(my_place + half - q, half)

    def along(t):
        return wrap(my_dp + t, dp)

    barrier = pltpu.get_barrier_semaphore()
    for k in range(1, subs):
        pl.semaphore_signal(barrier, inc=1, device_id=(my_dp, towards(k)), device_id_type=MESH)
    for t in range(1, dp):
        pl.semaphore_signal(barrier, inc=1, device_id=(along(t), my_sub), device_id_type=MESH)

    load_samples = pltpu.make_async_copy(samples_hbm, blocks.at[0], local_sem.at[0])
    load_codes = pltpu.make_async_copy(codebook_hbm.at[0], code_own, local_sem.at[1])
    load_rotation = pltpu.make_async_copy(rotation_hbm, rotation, local_sem.at[2])
    load_codes.start()
    load_samples.start()
    load_rotation.start()

    def remote(src, dst, send, recv, device):
        return pltpu.make_async_remote_copy(
            src_ref=src,
            dst_ref=dst,
            send_sem=send,
            recv_sem=recv,
            device_id=device,
            device_id_type=MESH,
        )

    def block_copy(k):
        return remote(
            samples_hbm, blocks.at[k], block_send.at[k], block_recv.at[k], (my_dp, towards(k))
        )

    pl.semaphore_wait(barrier, subs + dp - 2)
    for k in range(1, subs):
        block_copy(k).start()

    load_codes.wait()
    code_t = code_own[...]
    square = -0.5 * jnp.sum(code_t * code_t, axis=0, keepdims=True)
    high = square.astype(BF16).astype(F32)
    middle = (square - high).astype(BF16).astype(F32)
    low = square - high - middle
    row = lax.broadcasted_iota(jnp.int32, (16, codes), 0)
    split = jnp.where(row == 0, high, jnp.where(row == 1, middle, jnp.where(row == 2, low, 0.0)))
    code_tall[...] = jnp.concatenate([code_t, split], axis=0).T.astype(BF16)
    code_low = code_t.astype(BF16)
    load_rotation.wait()
    load_samples.wait()
    ones = jnp.ones((16, rows), BF16)

    sums = None
    cross = None
    for k in range(subs):
        if k > 0:
            block_copy(k).wait_recv()
        block = blocks[k]
        rotated = lax.dot_general(rotation[...], block, NT, preferred_element_type=F32).astype(BF16)
        wide = rotated.astype(F32)
        row_square = jnp.sum(wide * wide, axis=0, keepdims=True)
        tall = jnp.concatenate([rotated, ones], axis=0)
        inner = jnp.dot(code_tall[...], tall, preferred_element_type=F32)
        logits = -0.125 * (row_square - 2.0 * inner)
        powers = jnp.exp(logits - jnp.max(logits, axis=0, keepdims=True))
        weights = (powers * (1.0 / jnp.sum(powers, axis=0, keepdims=True))).astype(BF16)
        part = lax.dot_general(tall, weights, NT, preferred_element_type=F32)
        sums = part if sums is None else sums + part
        recon = jnp.dot(code_low, weights, preferred_element_type=F32).astype(BF16)
        part = jnp.dot(recon, block, preferred_element_type=F32)
        cross = part if cross is None else cross + part
        if k == 0:
            rec_in[my_sub] = recon
        else:
            rec_out[k] = recon

    pieces = sums[:width].reshape(dp, chunk, codes)
    pieces = jnp.concatenate([pieces[..., j : j + LANES] for j in range(0, codes, LANES)], axis=1)
    fill = pack_s.shape[1] - pieces.shape[1]
    if fill:
        pieces = jnp.concatenate([pieces, jnp.zeros((dp, fill, LANES), F32)], axis=1)
    pack_s[...] = pieces.astype(BF16)

    def spread(pack, two, t, s):
        return remote(
            pack.at[along(t)], two.at[t - 1], many_send.at[s], many_recv.at[s], (along(t), my_sub)
        )

    for t in range(1, dp):
        spread(pack_s, two_s, t, 0).start()

    tile = pack_x.shape[1]
    pieces = cross.T.reshape(dp, 2, tile, width)
    pack_x[...] = jnp.concatenate([pieces[:, 0], pieces[:, 1]], axis=2).astype(BF16)
    for t in range(1, dp):
        spread(pack_x, two_x, t, 1).start()

    count_out[...] = sums[width : width + 1]

    def send_count(t):
        return remote(
            count_out, count_in.at[my_dp], many_send.at[2], many_recv.at[2], (along(t), my_sub)
        )

    for t in range(1, dp):
        send_count(t).start()
    count_in[my_dp] = count_out[...]

    def send_recon(k):
        device = (my_dp, origin(k))
        return remote(rec_out.at[k], rec_in.at[my_sub], many_send.at[3], many_recv.at[3], device)

    for k in range(1, subs):
        send_recon(k).start()

    def bulk(buffer, count, s):
        part = buffer.at[pl.ds(0, count)]
        return remote(part, part, many_send.at[s], many_recv.at[s], (along(1), my_sub))

    bulk(two_s, dp - 1, 0).wait_recv()
    total = pack_s[my_dp].astype(F32) + jnp.sum(two_s[...].astype(F32), axis=0)
    own_total[...] = total.astype(BF16)

    def share(t):
        return remote(
            own_total, totals.at[my_dp], many_send.at[4], many_recv.at[4], (along(t), my_sub)
        )

    for t in range(1, dp):
        share(t).start()
    totals[my_dp] = own_total[...]

    bulk(two_x, dp - 1, 1).wait_recv()
    total_x = pack_x[my_dp].astype(F32) + jnp.sum(two_x[...].astype(F32), axis=0)
    total_x = jnp.concatenate([total_x[:, :width], total_x[:, width : 2 * width]], axis=0)
    cross_out[...] = jnp.concatenate([total_x, total_x], axis=1).reshape(cross_out.shape)

    def send_cross(k):
        peer = towards(k)
        return remote(
            cross_out.at[peer], cross_in.at[my_sub], many_send.at[5], many_recv.at[5], (my_dp, peer)
        )

    for k in range(1, subs):
        send_cross(k).start()
    cross_in[my_sub] = cross_out[my_sub]

    bulk(rec_in, subs - 1, 3).wait_recv()
    recon_ref[...] = rec_in[...].reshape(dim, rows).astype(F32).T.astype(BF16)

    bulk(count_in, dp - 1, 2).wait_recv()
    counts = 1.0 + jnp.sum(count_in[...], axis=0)
    bulk(totals, dp - 1, 4).wait_recv()
    all_totals = totals[...].astype(F32)
    for j in range(codes // LANES):
        lanes = slice(j * LANES, (j + 1) * LANES)
        part = all_totals[:, j * chunk : (j + 1) * chunk].reshape(width, LANES)
        new_ref[0, :, lanes] = (part + code_own[:, lanes]) / counts[:, lanes]

    bulk(cross_in, subs - 1, 5).wait_recv()
    cross_ref[...] = jnp.concatenate([cross_in[s][:, :width] for s in range(subs)], axis=1)

    for k in range(1, subs):
        block_copy(k).wait_send()
    bulk(two_s, dp - 1, 0).wait_send()
    bulk(two_x, dp - 1, 1).wait_send()
    bulk(count_in, dp - 1, 2).wait_send()
    bulk(rec_in, subs - 1, 3).wait_send()
    bulk(totals, dp - 1, 4).wait_send()
    bulk(cross_in, subs - 1, 5).wait_send()


def write_kernel(recon_ref, new_ref, cross_ref, recon_out, new_out, cross_out, sems):
    pairs = ((recon_ref, recon_out), (new_ref, new_out), (cross_ref, cross_out))
    copies = [pltpu.make_async_copy(s, d, sems.at[i]) for i, (s, d) in enumerate(pairs)]
    for copy in copies:
        copy.start()
    for copy in copies:
        copy.wait()


def per_device(dp, subs, samples, rotation, codebook):
    rows, dim = samples.shape
    codes, width = codebook.shape[1:]
    chunk = max(16, width * codes // (dp * LANES))
    out_rows = dim // (dp * subs)
    tile = dim // dp // 2
    dma = pltpu.SemaphoreType.DMA
    vmem = pl.BlockSpec(memory_space=pltpu.VMEM)
    hbm = pl.BlockSpec(memory_space=pltpu.HBM)
    shapes = (
        jax.ShapeDtypeStruct((rows, dim), BF16),
        jax.ShapeDtypeStruct((1, width, codes), F32),
        jax.ShapeDtypeStruct((out_rows, dim), F32),
    )
    parts = pl.pallas_call(
        functools.partial(kernel, dp, subs),
        out_shape=shapes,
        in_specs=[hbm] * 3,
        out_specs=(vmem,) * 3,
        scratch_shapes=[
            pltpu.VMEM((subs, rows, dim), BF16),
            pltpu.VMEM((width, dim), BF16),
            pltpu.VMEM((width, codes), F32),
            pltpu.VMEM((codes, width + 16), BF16),
            pltpu.VMEM((subs, width, rows), BF16),
            pltpu.VMEM((subs, width, rows), BF16),
            pltpu.VMEM((dp, chunk, LANES), BF16),
            pltpu.VMEM((dp, tile, LANES), BF16),
            pltpu.VMEM((dp - 1, chunk, LANES), BF16),
            pltpu.VMEM((dp - 1, tile, LANES), BF16),
            pltpu.VMEM((1, codes), F32),
            pltpu.VMEM((dp, 1, codes), F32),
            pltpu.VMEM((chunk, LANES), BF16),
            pltpu.VMEM((dp, chunk, LANES), BF16),
            pltpu.VMEM((subs, out_rows, LANES), F32),
            pltpu.VMEM((subs, out_rows, LANES), F32),
            dma((3,)),
            dma((subs,)),
            dma((subs,)),
            dma((6,)),
            dma((6,)),
        ],
        compiler_params=pltpu.CompilerParams(
            collective_id=0, has_side_effects=True, vmem_limit_bytes=40 * 1024 * 1024
        ),
    )(
        *(
            pltpu.with_memory_space_constraint(x, pltpu.HBM)
            for x in (samples, rotation.T, codebook.swapaxes(1, 2))
        )
    )
    recon, new_codes, cross = pl.pallas_call(
        write_kernel,
        out_shape=shapes,
        in_specs=[vmem] * 3,
        out_specs=(hbm,) * 3,
        scratch_shapes=[dma((3,))],
        compiler_params=pltpu.CompilerParams(vmem_limit_bytes=4 * 1024 * 1024),
    )(*parts)
    return recon, new_codes.swapaxes(1, 2), cross


def solution(mesh):
    in_specs = (P(("dp", "sub"), None), P(None, "sub"), P("sub", None, None))
    out_specs = (P(("dp", "sub"), None), P("sub", None, None), P(("dp", "sub"), None))
    return jax.shard_map(
        functools.partial(per_device, mesh.shape["dp"], mesh.shape["sub"]),
        mesh=mesh,
        in_specs=in_specs,
        out_specs=out_specs,
        check_vma=False,
    )
```

time: 182 us -> 21.1 us (0.12)
  waiting for transfers between devices: 113 us -> 0 us
  blocking collectives: 37.2 us -> 0 us
  Pallas kernels: 2.32 us -> 20.3 us
  between operations: 14.2 us -> 0.64 us
  starting transfers between devices: 6.74 us -> 0 us
  local copies, waits for them, and re-layouts: 4.53 us -> 0 us
    unnamed x2 -> x0, waiting for transfers between devices: 104 us -> none
    psum x1 -> x0, blocking collectives: 26.9 us -> none  [per_device(): lax.psum(sums.astype(jnp.bfloat16), 'dp').astype(jnp.float32)]
    pallas_call x0 -> x2, Pallas kernels: none -> 20.3 us  [the longest x1 19.6 us: per_device(): pl.pallas_call(functools.partial(kernel, dp, subs), out_shape=shapes, in_...]
    all_gather x1 -> x0, blocking collectives: 10.2 us -> none  [per_device(): full_rotation = lax.all_gather(rotation, 'sub', axis=1, tiled=True)]
    all_to_all x2 -> x0, waiting for transfers between devices: 9.12 us -> none  [the longest x1 4.59 us: per_device(): lax.all_to_all(rotated, 'sub', split_axis=1, concat_axis=0, tiled=True)]
    all_to_all x2 -> x0, starting transfers between devices: 6.7 us -> none  [the longest x1 3.42 us: per_device(): lax.all_to_all(rotated, 'sub', split_axis=1, concat_axis=0, tiled=True)]
    unnamed x16 -> x0, local copies, waits for them, and re-layouts: 2.95 us -> none
    unnamed x1 -> x0, Pallas kernels: 2.32 us -> none
  transfers between devices with their start and end apart: 3 -> 0, of which waited for: 3 -> 0; matrix products, arithmetic and copies ran while one was open for 1% -> 0% of each run, Pallas kernels for 0% -> 0%
where the time goes in v4:
time: 21.1 us; the launch traced here: 20.9 us
  Pallas kernels  20.3 us (96%)
  between operations  0.64 us (3%)
    pallas_call x1, Pallas kernels, per_device(): pl.pallas_call(functools.partial(kernel, dp, subs), out_shape=shapes, in_...  19.6 us
    pallas_call x1, Pallas kernels, per_device(): pl.pallas_call(write_kernel, out_shape=shapes, in_specs=[vmem] * 3, out_s...  0.68 us

profile of v4, /device:TPU:0, one launch (start us, length us, event | category | flops | bytes accessed | tf_op | source)
XLA Modules:
  0.0 20.9 jit_solution(5477516965409225127)
XLA Ops:
  0.6 19.6 %shard_map.58 = (bf16[128,256]{1,0:T(8,128)(2,1)S(1)}, f32[1,64,256]{2,1,0:T(8,128)S(1)}, f32[8,256]{1,0:T(8,128)S(1)}) custom-call(bf16[128,256]{1,0:T(8,128)(2,1)} %samples_hbm.1, bf16[64,256]{1,0:T(8,128)(2,1)} %bitcast.4, f32[1,64,256]{2,1,0:T(8,128)} %bitcast.3), custom_call_target="tpu_custom_call" | custom-call | tf_op jit(solution)/shard_map/pallas_call | solution.py:264
  20.3 0.7 %shard_map.59 = (bf16[128,256]{1,0:T(8,128)(2,1)}, f32[1,64,256]{2,1,0:T(8,128)}, f32[8,256]{1,0:T(8,128)}) custom-call(bf16[128,256]{1,0:T(8,128)(2,1)S(1)} %get-tuple-element.9.recon_ref, f32[1,64,256]{2,1,0:T(8,128)S(1)} %get-tuple-element.10.new_ref, f32[8,256]{1,0:T(8,128)S(1)} %get-tuple-element.11.cross_ref), custom_call_target="tpu_custom_call" | custom-call | tf_op jit(solution)/shard_map/pallas_call | solution.py:301

commit v5 on v4

--- a/solution.py
+++ b/solution.py
@@ -97,9 +97,10 @@
 
     def block_copy(k):
         return remote(
-            samples_hbm, blocks.at[k], block_send.at[k], block_recv.at[k], (my_dp, towards(k))
-        )
-
+            blocks.at[0], blocks.at[k], block_send.at[k], block_recv.at[k], (my_dp, towards(k))
+        )
+
+    load_samples.wait()
     pl.semaphore_wait(barrier, subs + dp - 2)
     for k in range(1, subs):
         block_copy(k).start()
@@ -115,32 +116,40 @@
     code_tall[...] = jnp.concatenate([code_t, split], axis=0).T.astype(BF16)
     code_low = code_t.astype(BF16)
     load_rotation.wait()
-    load_samples.wait()
-    ones = jnp.ones((16, rows), BF16)
-
-    sums = None
-    cross = None
-    for k in range(subs):
-        if k > 0:
+
+    def assign(first, count):
+        for k in range(max(first, 1), first + count):
             block_copy(k).wait_recv()
-        block = blocks[k]
+        block = blocks[first : first + count].reshape(count * rows, dim)
         rotated = lax.dot_general(rotation[...], block, NT, preferred_element_type=F32).astype(BF16)
         wide = rotated.astype(F32)
         row_square = jnp.sum(wide * wide, axis=0, keepdims=True)
-        tall = jnp.concatenate([rotated, ones], axis=0)
+        tall = jnp.concatenate([rotated, jnp.ones((16, count * rows), BF16)], axis=0)
         inner = jnp.dot(code_tall[...], tall, preferred_element_type=F32)
         logits = -0.125 * (row_square - 2.0 * inner)
         powers = jnp.exp(logits - jnp.max(logits, axis=0, keepdims=True))
         weights = (powers * (1.0 / jnp.sum(powers, axis=0, keepdims=True))).astype(BF16)
-        part = lax.dot_general(tall, weights, NT, preferred_element_type=F32)
-        sums = part if sums is None else sums + part
+        return weights, lax.dot_general(tall, weights, NT, preferred_element_type=F32), block
+
+    def rebuild(first, count, weights, block):
         recon = jnp.dot(code_low, weights, preferred_element_type=F32).astype(BF16)
-        part = jnp.dot(recon, block, preferred_element_type=F32)
-        cross = part if cross is None else cross + part
-        if k == 0:
-            rec_in[my_sub] = recon
-        else:
-            rec_out[k] = recon
+        for k in range(first, first + count):
+            piece = recon[:, (k - first) * rows : (k - first + 1) * rows]
+            if k == 0:
+                rec_in[my_sub] = piece
+            else:
+                rec_out[k] = piece
+        return jnp.dot(recon, block, preferred_element_type=F32)
+
+    groups = [(0, 1), (1, 1)] + [(k, 2) for k in range(2, subs, 2)]
+    sums = jnp.zeros((width + 16, codes), F32)
+    cross = jnp.zeros((width, dim), F32)
+    for first, count in groups[:-1]:
+        weights, part, block = assign(first, count)
+        sums += part
+        cross += rebuild(first, count, weights, block)
+    weights, part, block = assign(*groups[-1])
+    sums += part
 
     pieces = sums[:width].reshape(dp, chunk, codes)
     pieces = jnp.concatenate([pieces[..., j : j + LANES] for j in range(0, codes, LANES)], axis=1)
@@ -157,6 +166,7 @@
     for t in range(1, dp):
         spread(pack_s, two_s, t, 0).start()
 
+    cross += rebuild(*groups[-1], weights, block)
     tile = pack_x.shape[1]
     pieces = cross.T.reshape(dp, 2, tile, width)
     pack_x[...] = jnp.concatenate([pieces[:, 0], pieces[:, 1]], axis=2).astype(BF16)

time: 21.1 us -> 21 us (level)
  no operation moved by 1% of the time
where the time goes in v5:
time: 21 us; the launch traced here: 20.8 us
  Pallas kernels  20.2 us (96%)
  between operations  0.64 us (3%)
    pallas_call x1, Pallas kernels, per_device(): pl.pallas_call(functools.partial(kernel, dp, subs), out_shape=shapes, in_...  19.5 us
    pallas_call x1, Pallas kernels, per_device(): pl.pallas_call(write_kernel, out_shape=shapes, in_specs=[vmem] * 3, out_s...  0.68 us

profile of v5, /device:TPU:0, one launch (start us, length us, event | category | flops | bytes accessed | tf_op | source)
XLA Modules:
  0.0 20.8 jit_solution(10804694890281854123)
XLA Ops:
  0.6 19.5 %shard_map.58 = (bf16[128,256]{1,0:T(8,128)(2,1)S(1)}, f32[1,64,256]{2,1,0:T(8,128)S(1)}, f32[8,256]{1,0:T(8,128)S(1)}) custom-call(bf16[128,256]{1,0:T(8,128)(2,1)} %samples_hbm.1, bf16[64,256]{1,0:T(8,128)(2,1)} %bitcast.4, f32[1,64,256]{2,1,0:T(8,128)} %bitcast.3), custom_call_target="tpu_custom_call" | custom-call | tf_op jit(solution)/shard_map/pallas_call | solution.py:274
  20.2 0.7 %shard_map.59 = (bf16[128,256]{1,0:T(8,128)(2,1)}, f32[1,64,256]{2,1,0:T(8,128)}, f32[8,256]{1,0:T(8,128)}) custom-call(bf16[128,256]{1,0:T(8,128)(2,1)S(1)} %get-tuple-element.9.recon_ref, f32[1,64,256]{2,1,0:T(8,128)S(1)} %get-tuple-element.10.new_ref, f32[8,256]{1,0:T(8,128)S(1)} %get-tuple-element.11.cross_ref), custom_call_target="tpu_custom_call" | custom-call | tf_op jit(solution)/shard_map/pallas_call | solution.py:311

commit v6 on v5

--- a/solution.py
+++ b/solution.py
@@ -32,12 +32,13 @@
     rec_in,
     pack_s,
     pack_x,
+    one_s,
+    comb_s,
     two_s,
     two_x,
     count_out,
     count_in,
-    own_total,
-    totals,
+    new_all,
     cross_out,
     cross_in,
     local_sem,
@@ -53,7 +54,6 @@
     my_place = my_sub - my_part * half
     _, rows, dim = blocks.shape
     width, codes = code_own.shape
-    chunk = width // dp
     out_rows = cross_ref.shape[0]
 
     def wrap(index, count):
@@ -102,7 +102,7 @@
 
     load_samples.wait()
     pl.semaphore_wait(barrier, subs + dp - 2)
-    for k in range(1, subs):
+    for k in range(subs - 1, 0, -1):
         block_copy(k).start()
 
     load_codes.wait()
@@ -151,39 +151,48 @@
     weights, part, block = assign(*groups[-1])
     sums += part
 
-    pieces = sums[:width].reshape(dp, chunk, codes)
-    pieces = jnp.concatenate([pieces[..., j : j + LANES] for j in range(0, codes, LANES)], axis=1)
-    fill = pack_s.shape[1] - pieces.shape[1]
-    if fill:
-        pieces = jnp.concatenate([pieces, jnp.zeros((dp, fill, LANES), F32)], axis=1)
-    pack_s[...] = pieces.astype(BF16)
+    core = lax.rem(my_dp, 2)
+    my_z = my_dp // 2
+    partner = (my_dp + 1 - 2 * core, my_sub)
+    pack_s[...] = sums[:width].astype(BF16).reshape(pack_s.shape)
+    swap_s = remote(pack_s.at[1 - core], one_s, many_send.at[4], many_recv.at[4], partner)
+    swap_s.start()
+
+    count_out[...] = sums[width : width + 1]
+
+    def send_count(t):
+        return remote(
+            count_out, count_in.at[my_dp], many_send.at[2], many_recv.at[2], (along(t), my_sub)
+        )
+
+    for t in range(1, dp):
+        send_count(t).start()
+    count_in[my_dp] = count_out[...]
+
+    cross += rebuild(*groups[-1], weights, block)
+
+    swap_s.wait_recv()
+    comb_s[...] = (pack_s[core].astype(F32) + one_s[...].astype(F32)).astype(BF16)
+
+    def spread_s(t):
+        device = (2 * wrap(my_z + t, dp // 2) + core, my_sub)
+        return remote(comb_s, two_s.at[my_z], many_send.at[0], many_recv.at[0], device)
+
+    for t in range(1, dp // 2):
+        spread_s(t).start()
+    two_s[my_z] = comb_s[...]
 
     def spread(pack, two, t, s):
         return remote(
             pack.at[along(t)], two.at[t - 1], many_send.at[s], many_recv.at[s], (along(t), my_sub)
         )
 
-    for t in range(1, dp):
-        spread(pack_s, two_s, t, 0).start()
-
-    cross += rebuild(*groups[-1], weights, block)
     tile = pack_x.shape[1]
     pieces = cross.T.reshape(dp, 2, tile, width)
     pack_x[...] = jnp.concatenate([pieces[:, 0], pieces[:, 1]], axis=2).astype(BF16)
     for t in range(1, dp):
         spread(pack_x, two_x, t, 1).start()
 
-    count_out[...] = sums[width : width + 1]
-
-    def send_count(t):
-        return remote(
-            count_out, count_in.at[my_dp], many_send.at[2], many_recv.at[2], (along(t), my_sub)
-        )
-
-    for t in range(1, dp):
-        send_count(t).start()
-    count_in[my_dp] = count_out[...]
-
     def send_recon(k):
         device = (my_dp, origin(k))
         return remote(rec_out.at[k], rec_in.at[my_sub], many_send.at[3], many_recv.at[3], device)
@@ -195,18 +204,15 @@
         part = buffer.at[pl.ds(0, count)]
         return remote(part, part, many_send.at[s], many_recv.at[s], (along(1), my_sub))
 
-    bulk(two_s, dp - 1, 0).wait_recv()
-    total = pack_s[my_dp].astype(F32) + jnp.sum(two_s[...].astype(F32), axis=0)
-    own_total[...] = total.astype(BF16)
-
-    def share(t):
-        return remote(
-            own_total, totals.at[my_dp], many_send.at[4], many_recv.at[4], (along(t), my_sub)
-        )
-
-    for t in range(1, dp):
-        share(t).start()
-    totals[my_dp] = own_total[...]
+    bulk(count_in, dp - 1, 2).wait_recv()
+    counts = 1.0 + jnp.sum(count_in[...], axis=0)
+    bulk(two_s, dp // 2 - 1, 0).wait_recv()
+    mine = pl.ds(pl.multiple_of(core * (width // 2), width // 2), width // 2)
+    new_all[core] = (jnp.sum(two_s[...].astype(F32), axis=0) + code_own[mine]) / counts
+    swap_new = remote(
+        new_all.at[core], new_all.at[core], many_send.at[6], many_recv.at[6], partner
+    )
+    swap_new.start()
 
     bulk(two_x, dp - 1, 1).wait_recv()
     total_x = pack_x[my_dp].astype(F32) + jnp.sum(two_x[...].astype(F32), axis=0)
@@ -226,25 +232,20 @@
     bulk(rec_in, subs - 1, 3).wait_recv()
     recon_ref[...] = rec_in[...].reshape(dim, rows).astype(F32).T.astype(BF16)
 
-    bulk(count_in, dp - 1, 2).wait_recv()
-    counts = 1.0 + jnp.sum(count_in[...], axis=0)
-    bulk(totals, dp - 1, 4).wait_recv()
-    all_totals = totals[...].astype(F32)
-    for j in range(codes // LANES):
-        lanes = slice(j * LANES, (j + 1) * LANES)
-        part = all_totals[:, j * chunk : (j + 1) * chunk].reshape(width, LANES)
-        new_ref[0, :, lanes] = (part + code_own[:, lanes]) / counts[:, lanes]
+    swap_new.wait_recv()
+    new_ref[0] = new_all[...].reshape(width, codes)
 
     bulk(cross_in, subs - 1, 5).wait_recv()
     cross_ref[...] = jnp.concatenate([cross_in[s][:, :width] for s in range(subs)], axis=1)
 
     for k in range(1, subs):
         block_copy(k).wait_send()
-    bulk(two_s, dp - 1, 0).wait_send()
+    swap_s.wait_send()
+    swap_new.wait_send()
+    bulk(two_s, dp // 2 - 1, 0).wait_send()
     bulk(two_x, dp - 1, 1).wait_send()
     bulk(count_in, dp - 1, 2).wait_send()
     bulk(rec_in, subs - 1, 3).wait_send()
-    bulk(totals, dp - 1, 4).wait_send()
     bulk(cross_in, subs - 1, 5).wait_send()
 
 
@@ -260,7 +261,6 @@
 def per_device(dp, subs, samples, rotation, codebook):
     rows, dim = samples.shape
     codes, width = codebook.shape[1:]
-    chunk = max(16, width * codes // (dp * LANES))
     out_rows = dim // (dp * subs)
     tile = dim // dp // 2
     dma = pltpu.SemaphoreType.DMA
@@ -283,21 +283,22 @@
             pltpu.VMEM((codes, width + 16), BF16),
             pltpu.VMEM((subs, width, rows), BF16),
             pltpu.VMEM((subs, width, rows), BF16),
-            pltpu.VMEM((dp, chunk, LANES), BF16),
+            pltpu.VMEM((2, width // 2, codes), BF16),
             pltpu.VMEM((dp, tile, LANES), BF16),
-            pltpu.VMEM((dp - 1, chunk, LANES), BF16),
+            pltpu.VMEM((width // 2, codes), BF16),
+            pltpu.VMEM((width // 2, codes), BF16),
+            pltpu.VMEM((dp // 2, width // 2, codes), BF16),
             pltpu.VMEM((dp - 1, tile, LANES), BF16),
             pltpu.VMEM((1, codes), F32),
             pltpu.VMEM((dp, 1, codes), F32),
-            pltpu.VMEM((chunk, LANES), BF16),
-            pltpu.VMEM((dp, chunk, LANES), BF16),
+            pltpu.VMEM((2, width // 2, codes), F32),
             pltpu.VMEM((subs, out_rows, LANES), F32),
             pltpu.VMEM((subs, out_rows, LANES), F32),
             dma((3,)),
             dma((subs,)),
             dma((subs,)),
-            dma((6,)),
-            dma((6,)),
+            dma((7,)),
+            dma((7,)),
         ],
         compiler_params=pltpu.CompilerParams(
             collective_id=0, has_side_effects=True, vmem_limit_bytes=40 * 1024 * 1024

time: 21 us -> 21.2 us (level)
  no operation moved by 1% of the time
where the time goes in v6:
time: 21.2 us; the launch traced here: 21 us
  Pallas kernels  20.4 us (96%)
  between operations  0.64 us (3%)
    pallas_call x1, Pallas kernels, per_device(): pl.pallas_call(functools.partial(kernel, dp, subs), out_shape=shapes, in_...  19.7 us
    pallas_call x1, Pallas kernels, per_device(): pl.pallas_call(write_kernel, out_shape=shapes, in_specs=[vmem] * 3, out_s...  0.68 us

profile of v6, /device:TPU:0, one launch (start us, length us, event | category | flops | bytes accessed | tf_op | source)
XLA Modules:
  0.0 21.0 jit_solution(5254993097694729459)
XLA Ops:
  0.6 19.7 %shard_map.58 = (bf16[128,256]{1,0:T(8,128)(2,1)S(1)}, f32[1,64,256]{2,1,0:T(8,128)S(1)}, f32[8,256]{1,0:T(8,128)S(1)}) custom-call(bf16[128,256]{1,0:T(8,128)(2,1)} %samples_hbm.1, bf16[64,256]{1,0:T(8,128)(2,1)} %bitcast.4, f32[1,64,256]{2,1,0:T(8,128)} %bitcast.3), custom_call_target="tpu_custom_call" | custom-call | tf_op jit(solution)/shard_map/pallas_call | solution.py:274
  20.3 0.7 %shard_map.59 = (bf16[128,256]{1,0:T(8,128)(2,1)}, f32[1,64,256]{2,1,0:T(8,128)}, f32[8,256]{1,0:T(8,128)}) custom-call(bf16[128,256]{1,0:T(8,128)(2,1)S(1)} %get-tuple-element.9.recon_ref, f32[1,64,256]{2,1,0:T(8,128)S(1)} %get-tuple-element.10.new_ref, f32[8,256]{1,0:T(8,128)S(1)} %get-tuple-element.11.cross_ref), custom_call_target="tpu_custom_call" | custom-call | tf_op jit(solution)/shard_map/pallas_call | solution.py:312

commit v7 on v5

--- a/solution.py
+++ b/solution.py
@@ -15,16 +15,70 @@
 TN = (((0,), (0,)), ((), ()))
 
 
+def peers(subs):
+    half = subs // 2
+    my_sub = lax.axis_index("sub")
+    my_part = my_sub // half
+    my_place = my_sub - my_part * half
+
+    def wrap(index, count):
+        return jnp.where(index >= count, index - count, index)
+
+    steps = [(p, q) for p in range(2) for q in range(half)]
+
+    def towards(k):
+        p, q = steps[k]
+        return wrap(my_part + p, 2) * half + wrap(my_place + q, half)
+
+    def origin(k):
+        p, q = steps[k]
+        return wrap(my_part + 2 - p, 2) * half + wrap(my_place + half - q, half)
+
+    return wrap, towards, origin
+
+
+def remote(src, dst, send, recv, device):
+    return pltpu.make_async_remote_copy(
+        src_ref=src,
+        dst_ref=dst,
+        send_sem=send,
+        recv_sem=recv,
+        device_id=device,
+        device_id_type=MESH,
+    )
+
+
+def gather_kernel(subs, samples_hbm, blocks, local_sem, block_send, block_recv):
+    my_dp = lax.axis_index("dp")
+    _, towards, _ = peers(subs)
+    barrier = pltpu.get_barrier_semaphore()
+    for k in range(1, subs):
+        pl.semaphore_signal(barrier, inc=1, device_id=(my_dp, towards(k)), device_id_type=MESH)
+    load = pltpu.make_async_copy(samples_hbm, blocks.at[0], local_sem)
+    load.start()
+    load.wait()
+    pl.semaphore_wait(barrier, subs - 1)
+    copies = [
+        remote(
+            blocks.at[0], blocks.at[k], block_send.at[k], block_recv.at[k], (my_dp, towards(k))
+        )
+        for k in range(subs - 1, 0, -1)
+    ]
+    for copy in copies:
+        copy.start()
+    for copy in copies:
+        copy.wait()
+
+
 def kernel(
     dp,
     subs,
-    samples_hbm,
+    blocks,
     rotation_hbm,
     codebook_hbm,
     recon_ref,
     new_ref,
     cross_ref,
-    blocks,
     rotation,
     code_own,
     code_tall,
@@ -41,34 +95,17 @@
     cross_out,
     cross_in,
     local_sem,
-    block_send,
-    block_recv,
     many_send,
     many_recv,
 ):
-    half = subs // 2
     my_dp = lax.axis_index("dp")
     my_sub = lax.axis_index("sub")
-    my_part = my_sub // half
-    my_place = my_sub - my_part * half
+    wrap, towards, origin = peers(subs)
     _, rows, dim = blocks.shape
     width, codes = code_own.shape
     chunk = width // dp
     out_rows = cross_ref.shape[0]
 
-    def wrap(index, count):
-        return jnp.where(index >= count, index - count, index)
-
-    steps = [(p, q) for p in range(2) for q in range(half)]
-
-    def towards(k):
-        p, q = steps[k]
-        return wrap(my_part + p, 2) * half + wrap(my_place + q, half)
-
-    def origin(k):
-        p, q = steps[k]
-        return wrap(my_part + 2 - p, 2) * half + wrap(my_place + half - q, half)
-
     def along(t):
         return wrap(my_dp + t, dp)
 
@@ -78,32 +115,10 @@
     for t in range(1, dp):
         pl.semaphore_signal(barrier, inc=1, device_id=(along(t), my_sub), device_id_type=MESH)
 
-    load_samples = pltpu.make_async_copy(samples_hbm, blocks.at[0], local_sem.at[0])
     load_codes = pltpu.make_async_copy(codebook_hbm.at[0], code_own, local_sem.at[1])
     load_rotation = pltpu.make_async_copy(rotation_hbm, rotation, local_sem.at[2])
     load_codes.start()
-    load_samples.start()
     load_rotation.start()
-
-    def remote(src, dst, send, recv, device):
-        return pltpu.make_async_remote_copy(
-            src_ref=src,
-            dst_ref=dst,
-            send_sem=send,
-            recv_sem=recv,
-            device_id=device,
-            device_id_type=MESH,
-        )
-
-    def block_copy(k):
-        return remote(
-            blocks.at[0], blocks.at[k], block_send.at[k], block_recv.at[k], (my_dp, towards(k))
-        )
-
-    load_samples.wait()
-    pl.semaphore_wait(barrier, subs + dp - 2)
-    for k in range(1, subs):
-        block_copy(k).start()
 
     load_codes.wait()
     code_t = code_own[...]
@@ -118,8 +133,6 @@
     load_rotation.wait()
 
     def assign(first, count):
-        for k in range(max(first, 1), first + count):
-            block_copy(k).wait_recv()
         block = blocks[first : first + count].reshape(count * rows, dim)
         rotated = lax.dot_general(rotation[...], block, NT, preferred_element_type=F32).astype(BF16)
         wide = rotated.astype(F32)
@@ -141,7 +154,7 @@
                 rec_out[k] = piece
         return jnp.dot(recon, block, preferred_element_type=F32)
 
-    groups = [(0, 1), (1, 1)] + [(k, 2) for k in range(2, subs, 2)]
+    groups = [(k, 2) for k in range(0, subs, 2)]
     sums = jnp.zeros((width + 16, codes), F32)
     cross = jnp.zeros((width, dim), F32)
     for first, count in groups[:-1]:
@@ -163,6 +176,7 @@
             pack.at[along(t)], two.at[t - 1], many_send.at[s], many_recv.at[s], (along(t), my_sub)
         )
 
+    pl.semaphore_wait(barrier, subs + dp - 2)
     for t in range(1, dp):
         spread(pack_s, two_s, t, 0).start()
 
@@ -238,8 +252,6 @@
     bulk(cross_in, subs - 1, 5).wait_recv()
     cross_ref[...] = jnp.concatenate([cross_in[s][:, :width] for s in range(subs)], axis=1)
 
-    for k in range(1, subs):
-        block_copy(k).wait_send()
     bulk(two_s, dp - 1, 0).wait_send()
     bulk(two_x, dp - 1, 1).wait_send()
     bulk(count_in, dp - 1, 2).wait_send()
@@ -271,13 +283,22 @@
         jax.ShapeDtypeStruct((1, width, codes), F32),
         jax.ShapeDtypeStruct((out_rows, dim), F32),
     )
+    blocks = pl.pallas_call(
+        functools.partial(gather_kernel, subs),
+        out_shape=jax.ShapeDtypeStruct((subs, rows, dim), BF16),
+        in_specs=[hbm],
+        out_specs=vmem,
+        scratch_shapes=[dma, dma((subs,)), dma((subs,))],
+        compiler_params=pltpu.CompilerParams(
+            collective_id=0, has_side_effects=True, vmem_limit_bytes=16 * 1024 * 1024
+        ),
+    )(pltpu.with_memory_space_constraint(samples, pltpu.HBM))
     parts = pl.pallas_call(
         functools.partial(kernel, dp, subs),
         out_shape=shapes,
-        in_specs=[hbm] * 3,
+        in_specs=[vmem, hbm, hbm],
         out_specs=(vmem,) * 3,
         scratch_shapes=[
-            pltpu.VMEM((subs, rows, dim), BF16),
             pltpu.VMEM((width, dim), BF16),
             pltpu.VMEM((width, codes), F32),
             pltpu.VMEM((codes, width + 16), BF16),
@@ -294,19 +315,16 @@
             pltpu.VMEM((subs, out_rows, LANES), F32),
             pltpu.VMEM((subs, out_rows, LANES), F32),
             dma((3,)),
-            dma((subs,)),
-            dma((subs,)),
             dma((6,)),
             dma((6,)),
         ],
         compiler_params=pltpu.CompilerParams(
-            collective_id=0, has_side_effects=True, vmem_limit_bytes=40 * 1024 * 1024
+            collective_id=1, has_side_effects=True, vmem_limit_bytes=40 * 1024 * 1024
         ),
     )(
-        *(
-            pltpu.with_memory_space_constraint(x, pltpu.HBM)
-            for x in (samples, rotation.T, codebook.swapaxes(1, 2))
-        )
+        blocks,
+        pltpu.with_memory_space_constraint(rotation.T, pltpu.HBM),
+        pltpu.with_memory_space_constraint(codebook.swapaxes(1, 2), pltpu.HBM),
     )
     recon, new_codes, cross = pl.pallas_call(
         write_kernel,

time: 21 us -> 20.8 us (level)
  Pallas kernels: 20.2 us -> 19.9 us
    pallas_call x1, Pallas kernels: 19.5 us -> 11.4 us  [per_device(): pl.pallas_call(functools.partial(kernel, dp, subs), out_shape=shapes, in_...]
    pallas_call x0 -> x1, Pallas kernels: none -> 7.8 us  [per_device(): pl.pallas_call(functools.partial(gather_kernel, subs), out_shape=jax.Shap...]
where the time goes in v7:
time: 20.8 us; the launch traced here: 20.6 us
  Pallas kernels  19.9 us (96%)
  between operations  0.65 us (3%)
    pallas_call x1, Pallas kernels, per_device(): pl.pallas_call(functools.partial(kernel, dp, subs), out_shape=shapes, in_...  11.4 us
    pallas_call x1, Pallas kernels, per_device(): pl.pallas_call(functools.partial(gather_kernel, subs), out_shape=jax.Shap...  7.8 us
    pallas_call x1, Pallas kernels, per_device(): pl.pallas_call(write_kernel, out_shape=shapes, in_specs=[vmem] * 3, out_s...  0.68 us

profile of v7, /device:TPU:0, one launch (start us, length us, event | category | flops | bytes accessed | tf_op | source)
XLA Modules:
  0.0 20.6 jit_solution(15729068315532458355)
XLA Ops:
  0.6 7.8 %shard_map.58.blocks = bf16[4,128,256]{2,1,0:T(8,128)(2,1)S(1)} custom-call(bf16[128,256]{1,0:T(8,128)(2,1)} %samples_hbm.1), custom_call_target="tpu_custom_call" | custom-call | tf_op jit(solution)/shard_map/pallas_call | solution.py:286
  8.4 11.4 %shard_map.59 = (bf16[128,256]{1,0:T(8,128)(2,1)S(1)}, f32[1,64,256]{2,1,0:T(8,128)S(1)}, f32[8,256]{1,0:T(8,128)S(1)}) custom-call(bf16[4,128,256]{2,1,0:T(8,128)(2,1)S(1)} %shard_map.58.blocks, bf16[64,256]{1,0:T(8,128)(2,1)} %bitcast.4, f32[1,64,256]{2,1,0:T(8,128)} %bitcast.3), custom_call_target="tpu_custom_call" | custom-call | tf_op jit(solution)/shard_map/pallas_call | solution.py:296
  19.9 0.7 %shard_map.60 = (bf16[128,256]{1,0:T(8,128)(2,1)}, f32[1,64,256]{2,1,0:T(8,128)}, f32[8,256]{1,0:T(8,128)}) custom-call(bf16[128,256]{1,0:T(8,128)(2,1)S(1)} %get-tuple-element.9.recon_ref, f32[1,64,256]{2,1,0:T(8,128)S(1)} %get-tuple-element.10.new_ref, f32[8,256]{1,0:T(8,128)S(1)} %get-tuple-element.11.cross_ref), custom_call_target="tpu_custom_call" | custom-call | tf_op jit(solution)/shard_map/pallas_call | solution.py:329

commit v8 on v7

--- a/solution.py
+++ b/solution.py
@@ -48,40 +48,102 @@
     )
 
 
-def gather_kernel(subs, samples_hbm, blocks, local_sem, block_send, block_recv):
+def lengthen(code_t):
+    codes = code_t.shape[1]
+    square = -0.5 * jnp.sum(code_t * code_t, axis=0, keepdims=True)
+    high = square.astype(BF16).astype(F32)
+    middle = (square - high).astype(BF16).astype(F32)
+    low = square - high - middle
+    row = lax.broadcasted_iota(jnp.int32, (16, codes), 0)
+    split = jnp.where(row == 0, high, jnp.where(row == 1, middle, jnp.where(row == 2, low, 0.0)))
+    return jnp.concatenate([code_t, split], axis=0).T.astype(BF16)
+
+
+def assign(rotation, code_tall, block):
+    rotated = lax.dot_general(rotation, block, NT, preferred_element_type=F32).astype(BF16)
+    wide = rotated.astype(F32)
+    row_square = jnp.sum(wide * wide, axis=0, keepdims=True)
+    tall = jnp.concatenate([rotated, jnp.ones((16, block.shape[0]), BF16)], axis=0)
+    inner = jnp.dot(code_tall, tall, preferred_element_type=F32)
+    logits = -0.125 * (row_square - 2.0 * inner)
+    powers = jnp.exp(logits - jnp.max(logits, axis=0, keepdims=True))
+    weights = (powers * (1.0 / jnp.sum(powers, axis=0, keepdims=True))).astype(BF16)
+    return weights, lax.dot_general(tall, weights, NT, preferred_element_type=F32)
+
+
+def gather_kernel(
+    subs,
+    samples_hbm,
+    rotation_hbm,
+    codebook_hbm,
+    blocks,
+    rotation,
+    code_own,
+    code_tall,
+    rec,
+    sums_ref,
+    cross_ref,
+    local_sem,
+    block_send,
+    block_recv,
+):
     my_dp = lax.axis_index("dp")
     _, towards, _ = peers(subs)
     barrier = pltpu.get_barrier_semaphore()
     for k in range(1, subs):
         pl.semaphore_signal(barrier, inc=1, device_id=(my_dp, towards(k)), device_id_type=MESH)
-    load = pltpu.make_async_copy(samples_hbm, blocks.at[0], local_sem)
-    load.start()
-    load.wait()
+    load_samples = pltpu.make_async_copy(samples_hbm, blocks.at[0], local_sem.at[0])
+    load_codes = pltpu.make_async_copy(codebook_hbm.at[0], code_own, local_sem.at[1])
+    load_rotation = pltpu.make_async_copy(rotation_hbm, rotation, local_sem.at[2])
+    load_samples.start()
+    load_codes.start()
+    load_rotation.start()
+    load_samples.wait()
     pl.semaphore_wait(barrier, subs - 1)
     copies = [
         remote(
             blocks.at[0], blocks.at[k], block_send.at[k], block_recv.at[k], (my_dp, towards(k))
         )
-        for k in range(subs - 1, 0, -1)
+        for k in range(1, subs)
     ]
     for copy in copies:
         copy.start()
+    load_codes.wait()
+    load_rotation.wait()
+    code_tall[...] = lengthen(code_own[...])
+    code_low = code_own[...].astype(BF16)
+    for k in range(subs // 2):
+        if k > 0:
+            copies[k - 1].wait_recv()
+        weights, part = assign(rotation[...], code_tall[...], blocks[k])
+        recon = jnp.dot(code_low, weights, preferred_element_type=F32).astype(BF16)
+        rec[k] = recon
+        whole = jnp.dot(recon, blocks[k], preferred_element_type=F32)
+        if k == 0:
+            sums_ref[...] = part
+            cross_ref[...] = whole
+        else:
+            sums_ref[...] += part
+            cross_ref[...] += whole
+    for copy in copies[subs // 2 - 1 :]:
+        copy.wait_recv()
     for copy in copies:
-        copy.wait()
+        copy.wait_send()
 
 
 def kernel(
     dp,
     subs,
     blocks,
-    rotation_hbm,
-    codebook_hbm,
+    rotation,
+    code_own,
+    code_tall,
+    rec_first,
+    sums_first,
+    cross_first,
     recon_ref,
     new_ref,
     cross_ref,
-    rotation,
-    code_own,
-    code_tall,
     rec_out,
     rec_in,
     pack_s,
@@ -94,7 +156,6 @@
     totals,
     cross_out,
     cross_in,
-    local_sem,
     many_send,
     many_recv,
 ):
@@ -115,53 +176,29 @@
     for t in range(1, dp):
         pl.semaphore_signal(barrier, inc=1, device_id=(along(t), my_sub), device_id_type=MESH)
 
-    load_codes = pltpu.make_async_copy(codebook_hbm.at[0], code_own, local_sem.at[1])
-    load_rotation = pltpu.make_async_copy(rotation_hbm, rotation, local_sem.at[2])
-    load_codes.start()
-    load_rotation.start()
-
-    load_codes.wait()
-    code_t = code_own[...]
-    square = -0.5 * jnp.sum(code_t * code_t, axis=0, keepdims=True)
-    high = square.astype(BF16).astype(F32)
-    middle = (square - high).astype(BF16).astype(F32)
-    low = square - high - middle
-    row = lax.broadcasted_iota(jnp.int32, (16, codes), 0)
-    split = jnp.where(row == 0, high, jnp.where(row == 1, middle, jnp.where(row == 2, low, 0.0)))
-    code_tall[...] = jnp.concatenate([code_t, split], axis=0).T.astype(BF16)
-    code_low = code_t.astype(BF16)
-    load_rotation.wait()
-
-    def assign(first, count):
+    code_low = code_own[...].astype(BF16)
+
+    def work(first, count):
         block = blocks[first : first + count].reshape(count * rows, dim)
-        rotated = lax.dot_general(rotation[...], block, NT, preferred_element_type=F32).astype(BF16)
-        wide = rotated.astype(F32)
-        row_square = jnp.sum(wide * wide, axis=0, keepdims=True)
-        tall = jnp.concatenate([rotated, jnp.ones((16, count * rows), BF16)], axis=0)
-        inner = jnp.dot(code_tall[...], tall, preferred_element_type=F32)
-        logits = -0.125 * (row_square - 2.0 * inner)
-        powers = jnp.exp(logits - jnp.max(logits, axis=0, keepdims=True))
-        weights = (powers * (1.0 / jnp.sum(powers, axis=0, keepdims=True))).astype(BF16)
-        return weights, lax.dot_general(tall, weights, NT, preferred_element_type=F32), block
+        return *assign(rotation[...], code_tall[...], block), block
 
     def rebuild(first, count, weights, block):
         recon = jnp.dot(code_low, weights, preferred_element_type=F32).astype(BF16)
         for k in range(first, first + count):
-            piece = recon[:, (k - first) * rows : (k - first + 1) * rows]
-            if k == 0:
-                rec_in[my_sub] = piece
-            else:
-                rec_out[k] = piece
+            rec_out[k] = recon[:, (k - first) * rows : (k - first + 1) * rows]
         return jnp.dot(recon, block, preferred_element_type=F32)
 
-    groups = [(k, 2) for k in range(0, subs, 2)]
-    sums = jnp.zeros((width + 16, codes), F32)
-    cross = jnp.zeros((width, dim), F32)
+    rec_in[my_sub] = rec_first[0]
+    for k in range(1, subs // 2):
+        rec_out[k] = rec_first[k]
+    groups = [(k, 2) for k in range(subs // 2, subs, 2)]
+    sums = sums_first[...]
+    cross = cross_first[...]
     for first, count in groups[:-1]:
-        weights, part, block = assign(first, count)
+        weights, part, block = work(first, count)
         sums += part
         cross += rebuild(first, count, weights, block)
-    weights, part, block = assign(*groups[-1])
+    weights, part, block = work(*groups[-1])
     sums += part
 
     pieces = sums[:width].reshape(dp, chunk, codes)
@@ -283,25 +320,35 @@
         jax.ShapeDtypeStruct((1, width, codes), F32),
         jax.ShapeDtypeStruct((out_rows, dim), F32),
     )
-    blocks = pl.pallas_call(
+    first = pl.pallas_call(
         functools.partial(gather_kernel, subs),
-        out_shape=jax.ShapeDtypeStruct((subs, rows, dim), BF16),
-        in_specs=[hbm],
-        out_specs=vmem,
-        scratch_shapes=[dma, dma((subs,)), dma((subs,))],
+        out_shape=(
+            jax.ShapeDtypeStruct((subs, rows, dim), BF16),
+            jax.ShapeDtypeStruct((width, dim), BF16),
+            jax.ShapeDtypeStruct((width, codes), F32),
+            jax.ShapeDtypeStruct((codes, width + 16), BF16),
+            jax.ShapeDtypeStruct((subs // 2, width, rows), BF16),
+            jax.ShapeDtypeStruct((width + 16, codes), F32),
+            jax.ShapeDtypeStruct((width, dim), F32),
+        ),
+        in_specs=[hbm] * 3,
+        out_specs=(vmem,) * 7,
+        scratch_shapes=[dma((3,)), dma((subs,)), dma((subs,))],
         compiler_params=pltpu.CompilerParams(
-            collective_id=0, has_side_effects=True, vmem_limit_bytes=16 * 1024 * 1024
+            collective_id=0, has_side_effects=True, vmem_limit_bytes=40 * 1024 * 1024
         ),
-    )(pltpu.with_memory_space_constraint(samples, pltpu.HBM))
+    )(
+        *(
+            pltpu.with_memory_space_constraint(x, pltpu.HBM)
+            for x in (samples, rotation.T, codebook.swapaxes(1, 2))
+        )
+    )
     parts = pl.pallas_call(
         functools.partial(kernel, dp, subs),
         out_shape=shapes,
-        in_specs=[vmem, hbm, hbm],
+        in_specs=[vmem] * 7,
         out_specs=(vmem,) * 3,
         scratch_shapes=[
-            pltpu.VMEM((width, dim), BF16),
-            pltpu.VMEM((width, codes), F32),
-            pltpu.VMEM((codes, width + 16), BF16),
             pltpu.VMEM((subs, width, rows), BF16),
             pltpu.VMEM((subs, width, rows), BF16),
             pltpu.VMEM((dp, chunk, LANES), BF16),
@@ -314,18 +361,13 @@
             pltpu.VMEM((dp, chunk, LANES), BF16),
             pltpu.VMEM((subs, out_rows, LANES), F32),
             pltpu.VMEM((subs, out_rows, LANES), F32),
-            dma((3,)),
             dma((6,)),
             dma((6,)),
         ],
         compiler_params=pltpu.CompilerParams(
             collective_id=1, has_side_effects=True, vmem_limit_bytes=40 * 1024 * 1024
         ),
-    )(
-        blocks,
-        pltpu.with_memory_space_constraint(rotation.T, pltpu.HBM),
-        pltpu.with_memory_space_constraint(codebook.swapaxes(1, 2), pltpu.HBM),
-    )
+    )(*first)
     recon, new_codes, cross = pl.pallas_call(
         write_kernel,
         out_shape=shapes,

time: 20.8 us -> 21.2 us (1.019)
  Pallas kernels: 19.9 us -> 20.4 us
    pallas_call x1, Pallas kernels: 7.8 us -> 8.39 us  [per_device(): pl.pallas_call(functools.partial(gather_kernel, subs), out_shape=(jax.Sha...]
where the time goes in v8:
time: 21.2 us; the launch traced here: 21 us
  Pallas kernels  20.4 us (96%)
  between operations  0.65 us (3%)
    pallas_call x1, Pallas kernels, per_device(): pl.pallas_call(functools.partial(kernel, dp, subs), out_shape=shapes, in_...  11.3 us
    pallas_call x1, Pallas kernels, per_device(): pl.pallas_call(functools.partial(gather_kernel, subs), out_shape=(jax.Sha...  8.39 us
    pallas_call x1, Pallas kernels, per_device(): pl.pallas_call(write_kernel, out_shape=shapes, in_specs=[vmem] * 3, out_s...  0.68 us

profile of v8, /device:TPU:0, one launch (start us, length us, event | category | flops | bytes accessed | tf_op | source)
XLA Modules:
  0.0 21.0 jit_solution(15439877429594897269)
XLA Ops:
  0.6 8.4 %shard_map.58 = (bf16[4,128,256]{2,1,0:T(8,128)(2,1)S(1)}, bf16[64,256]{1,0:T(8,128)(2,1)S(1)}, f32[64,256]{1,0:T(8,128)S(1)}, bf16[256,80]{1,0:T(8,128)(2,1)S(1...) custom-call(bf16[128,256]{1,0:T(8,128)(2,1)} %samples_hbm.1, ...), custom_call_target="tpu_custom_call" | custom-call | tf_op jit(solution)/shard_map/pallas_call | solution.py:323
  9.0 11.3 %shard_map.59 = (bf16[128,256]{1,0:T(8,128)(2,1)S(1)}, f32[1,64,256]{2,1,0:T(8,128)S(1)}, f32[8,256]{1,0:T(8,128)S(1)}) custom-call(bf16[4,128,256]{2,1,0:T(8,128)(2,1)S(1)} %get-tuple-element.16.blocks, bf16[64,256]{1,0:T(8,128)(2,1)S(1)} %get-tuple-element.17.rotation, f32[64,256]{1,0:T(8,128)S(1)} %get-tuple-element.18.code_own, ...), custom_call_target="tpu_custom_call" | custom-call | tf_op jit(solution)/shard_map/pallas_call | solution.py:346
  20.3 0.7 %shard_map.60 = (bf16[128,256]{1,0:T(8,128)(2,1)}, f32[1,64,256]{2,1,0:T(8,128)}, f32[8,256]{1,0:T(8,128)}) custom-call(bf16[128,256]{1,0:T(8,128)(2,1)S(1)} %get-tuple-element.23.recon_ref, f32[1,64,256]{2,1,0:T(8,128)S(1)} %get-tuple-element.24.new_ref, f32[8,256]{1,0:T(8,128)S(1)} %get-tuple-element.25.cross_ref), custom_call_target="tpu_custom_call" | custom-call | tf_op jit(solution)/shard_map/pallas_call | solution.py:371

commit v9 on v5

--- a/solution.py
+++ b/solution.py
@@ -73,10 +73,10 @@
         return wrap(my_dp + t, dp)
 
     barrier = pltpu.get_barrier_semaphore()
+    for t in range(1, dp):
+        pl.semaphore_signal(barrier, inc=1, device_id=(along(t), my_sub), device_id_type=MESH)
     for k in range(1, subs):
         pl.semaphore_signal(barrier, inc=1, device_id=(my_dp, towards(k)), device_id_type=MESH)
-    for t in range(1, dp):
-        pl.semaphore_signal(barrier, inc=1, device_id=(along(t), my_sub), device_id_type=MESH)
 
     load_samples = pltpu.make_async_copy(samples_hbm, blocks.at[0], local_sem.at[0])
     load_codes = pltpu.make_async_copy(codebook_hbm.at[0], code_own, local_sem.at[1])
@@ -102,7 +102,7 @@
 
     load_samples.wait()
     pl.semaphore_wait(barrier, subs + dp - 2)
-    for k in range(1, subs):
+    for k in range(subs - 1, 0, -1):
         block_copy(k).start()
 
     load_codes.wait()

time: 21 us -> 20.6 us (0.981)
  Pallas kernels: 20.2 us -> 19.8 us
    pallas_call x1, Pallas kernels: 19.5 us -> 19.2 us  [per_device(): pl.pallas_call(functools.partial(kernel, dp, subs), out_shape=shapes, in_...]
where the time goes in v9:
time: 20.6 us; the launch traced here: 20.5 us
  Pallas kernels  19.8 us (96%)
  between operations  0.64 us (3%)
    pallas_call x1, Pallas kernels, per_device(): pl.pallas_call(functools.partial(kernel, dp, subs), out_shape=shapes, in_...  19.2 us
    pallas_call x1, Pallas kernels, per_device(): pl.pallas_call(write_kernel, out_shape=shapes, in_specs=[vmem] * 3, out_s...  0.68 us

profile of v9, /device:TPU:0, one launch (start us, length us, event | category | flops | bytes accessed | tf_op | source)
XLA Modules:
  0.0 20.5 jit_solution(9106810382139376631)
XLA Ops:
  0.6 19.2 %shard_map.58 = (bf16[128,256]{1,0:T(8,128)(2,1)S(1)}, f32[1,64,256]{2,1,0:T(8,128)S(1)}, f32[8,256]{1,0:T(8,128)S(1)}) custom-call(bf16[128,256]{1,0:T(8,128)(2,1)} %samples_hbm.1, bf16[64,256]{1,0:T(8,128)(2,1)} %bitcast.4, f32[1,64,256]{2,1,0:T(8,128)} %bitcast.3), custom_call_target="tpu_custom_call" | custom-call | tf_op jit(solution)/shard_map/pallas_call | solution.py:274
  19.8 0.7 %shard_map.59 = (bf16[128,256]{1,0:T(8,128)(2,1)}, f32[1,64,256]{2,1,0:T(8,128)}, f32[8,256]{1,0:T(8,128)}) custom-call(bf16[128,256]{1,0:T(8,128)(2,1)S(1)} %get-tuple-element.9.recon_ref, f32[1,64,256]{2,1,0:T(8,128)S(1)} %get-tuple-element.10.new_ref, f32[8,256]{1,0:T(8,128)S(1)} %get-tuple-element.11.cross_ref), custom_call_target="tpu_custom_call" | custom-call | tf_op jit(solution)/shard_map/pallas_call | solution.py:311
